TPU v7x, 32 devices: a whole 2x2x4 slice. The times are simulated.
32 devices in a mesh: seq: 4 (over y, x), head: 8 (over z, core).
Axes of the slice: x: 2, y: 2, z: 4, core: 2. Of those that a mesh axis runs over, the one named last changes fastest.
Arguments:
- tokens: bfloat16 [2, 4096, 4096], P(None, 'seq', 'head'), may hold values from -6 to 6
- w_gate: bfloat16 [4096, 2048], P(None, 'head'), may hold values from -0.09375 to 0.09375
- w_value: bfloat16 [4096, 2048], P(None, 'head'), may hold values from -0.09375 to 0.09375
- w_bc: bfloat16 [4096, 256], replicated, may hold values from -0.09375 to 0.09375
- w_step: bfloat16 [4096, 32], P(None, 'head'), may hold values from -0.09375 to 0.09375
- step_bias: float32 [32], P('head'), may hold values from -1 to 1
- rate: float32 [32], P('head'), may hold values from 1.2207031e-05 to 0.1
- conv_value: float32 [4, 2048], P(None, 'head'), may hold values from -3 to 3
- conv_bc: float32 [4, 256], replicated, may hold values from -3 to 3
- norm_gain: float32 [2048], P('head'), may hold values from 0.5 to 1.5
- w_out: bfloat16 [2048, 4096], P('head'), may hold values from -0.1875 to 0.1875
- kept_states: float32 [32, 32, 64, 128], P('seq', 'head'), may hold values from -2.4 to 2.4
- kept_index: int32 [2], replicated, may hold values from 0 to 31
- cached_len: int32 [2], replicated, may hold values from 0 to 4095
Outputs:
- mixed: bfloat16 [2, 4096, 4096], P(None, 'seq', 'head')
Inputs may be any that keep to these rules, and one draw needn't show every extreme that they name: Prompt b starts from kept state kept_index[b]; positions below cached_len[b] are already folded into that state.
All inputs are finite; a program needn't handle non-finite values.
Results may differ from a plain program's by a relative error of at most 0.028.
Values may be sent and summed in bfloat16 or wider, within the bound.
A program may use at most 128 MiB of HBM per device.

v0:
```python
import jax
import jax.numpy as jnp
from jax import lax
from jax.sharding import PartitionSpec as P

CONV = 4


def passed_along(block, axis, distance):
    devices = range(lax.axis_size(axis))
    route = [(i - distance, i) for i in devices if i - distance in devices]
    return lax.ppermute(block, axis, route)


def for_sending(shard):

    def short(part):
        return part.astype(jnp.bfloat16) if part.dtype == jnp.float32 else part

    return jax.tree.map(short, shard)


def from_root(block, axis, source):
    block = jnp.where(lax.axis_index(axis) == source, block, jnp.zeros_like(block))
    return lax.psum(block, axis)


def combine(earlier, later):
    return (earlier[0] * later[0], later[0][:, :, None, None] * earlier[1] + later[1])


def per_device(
    tokens,
    w_gate,
    w_value,
    w_bc,
    w_step,
    step_bias,
    rate,
    conv_value,
    conv_bc,
    norm_gain,
    w_out,
    kept_states,
    kept_index,
    cached_len,
):
    batch, sec_len, d_part = tokens.shape
    inner_dev = w_gate.shape[1]
    heads_dev = w_step.shape[1]
    head_size = inner_dev // heads_dev
    state_size = w_bc.shape[1] // 2
    slots = kept_states.shape[0]
    weights = jnp.concatenate([w_gate, w_value, w_bc, w_step], axis=1)
    width = weights.shape[1]
    piece = lax.all_gather(tokens, "head", axis=2, tiled=True)
    proj = jnp.dot(piece.reshape(-1, piece.shape[2]), weights, preferred_element_type=jnp.float32)
    proj = proj.astype(jnp.bfloat16).reshape(batch, sec_len, width)
    gate = proj[:, :, :inner_dev]
    bc_end = 2 * inner_dev + 2 * state_size
    mixin = proj[:, :, inner_dev:bc_end]
    step_raw = proj[:, :, bc_end:]
    tail = mixin[:, sec_len - (CONV - 1) :, :]
    previous = passed_along(tail, "seq", 1)
    padded = jnp.concatenate([previous, mixin], axis=1).astype(jnp.float32)
    taps = jnp.concatenate([conv_value, conv_bc], axis=1)
    conv = jnp.zeros((batch, sec_len, taps.shape[1]), jnp.float32)
    for k in range(CONV):
        conv = conv + taps[k][None, None, :] * padded[:, k : k + sec_len, :]
    conv = jax.nn.silu(conv)
    xs = conv[:, :, :inner_dev].reshape(batch, sec_len, heads_dev, head_size)
    bmat = conv[:, :, inner_dev : inner_dev + state_size]
    cmat = conv[:, :, inner_dev + state_size :]
    positions = lax.axis_index("seq") * sec_len + jnp.arange(sec_len, dtype=jnp.int32)
    mask = (positions[None, :] >= cached_len[:, None]).astype(jnp.float32)
    dt = jax.nn.softplus(step_raw.astype(jnp.float32) + step_bias[None, None, :]) * mask[:, :, None]
    cumul = jnp.cumsum(-dt * rate[None, None, :], axis=1)
    cumul_t = cumul.transpose(0, 2, 1)
    drive = dt[:, :, :, None] * xs
    high = lax.Precision.HIGHEST
    scores = jnp.einsum("bin,bjn->bij", cmat, bmat, precision=high)
    later_idx = jnp.arange(sec_len, dtype=jnp.int32)
    lower = (later_idx[:, None] >= later_idx[None, :]).astype(jnp.float32)
    diffs = cumul_t[:, :, :, None] - cumul_t[:, :, None, :]
    weighting = jnp.exp(jnp.minimum(diffs, 0.0)) * lower[None, None] * scores[:, None]
    y_local = jnp.einsum("bhij,bjhp->bihp", weighting, drive, precision=high)
    to_end = jnp.exp(cumul_t[:, :, -1:] - cumul_t)
    sec_state = jnp.einsum("bhj,bjhp,bjn->bhpn", to_end, drive, bmat, precision=high)
    sec_decay = jnp.exp(cumul_t[:, :, -1])
    ones = jnp.ones_like(sec_decay)
    zeros = jnp.zeros_like(sec_state)
    first = lax.axis_index("seq") == 0
    before_decay, before_state = (ones, zeros)
    for turn in range(lax.axis_size("seq") - 1):
        outgoing = combine((before_decay, before_state), (sec_decay, sec_state))
        got_decay, got_state = passed_along(
            (for_sending(outgoing[0]), for_sending(outgoing[1])), "seq", 1
        )
        before_decay = jnp.where(first, ones, got_decay)
        before_state = got_state
    picked = kept_states[kept_index % slots]
    owners = kept_index // slots
    start_state = jnp.stack(
        [
            from_root(picked[b].astype(jnp.bfloat16), "seq", owners[b]).astype(jnp.float32)
            for b in range(batch)
        ],
        axis=0,
    )
    incoming = before_decay[:, :, None, None] * start_state + before_state
    y_carry = (
        jnp.einsum("bhpn,bin->bihp", incoming, cmat, precision=high) * jnp.exp(cumul)[:, :, :, None]
    )
    y = y_local + y_carry
    y = (y * mask[:, :, None, None]).reshape(batch * sec_len, inner_dev)
    gated = y * jax.nn.silu(gate.reshape(batch * sec_len, inner_dev).astype(jnp.float32))
    squares = lax.psum(jnp.sum(gated * gated, axis=1), "head")
    meansq = squares / (inner_dev * lax.axis_size("head"))
    normed = (gated * lax.rsqrt(meansq + 1e-05)[:, None] * norm_gain[None, :]).astype(jnp.bfloat16)
    summed = lax.psum_scatter(
        lax.dot_general(
            w_out, normed, (((0,), (1,)), ((), ())), preferred_element_type=jnp.float32
        ).astype(jnp.bfloat16),
        "head",
        scatter_dimension=0,
        tiled=True,
    ).astype(jnp.float32)
    return summed.T.astype(jnp.bfloat16).reshape(batch, sec_len, d_part)


def solution(mesh):
    return jax.shard_map(
        per_device,
        mesh=mesh,
        in_specs=(
            P(None, "seq", "head"),
            P(None, "head"),
            P(None, "head"),
            P(),
            P(None, "head"),
            P("head"),
            P("head"),
            P(None, "head"),
            P(),
            P("head"),
            P("head", None),
            P("seq", "head", None, None),
            P(),
            P(),
        ),
        out_specs=P(None, "seq", "head"),
        check_vma=False,
    )
```

profile of v0, /device:TPU:6, one launch (start us, length us, event | category | flops | bytes accessed | tf_op | source)
XLA Modules:
  0.0 525.9 jit_solution(13374605982386123591)
XLA Ops:
  10.6 1.8 gather_fusion
  13.1 2.5 fusion.22
  16.3 145.8 %all-gather.2.cloned.1.call-done = bf16[2,1024,4096]{2,1,0:T(8,128)(2,1)} async-done(((bf16[2,1024,512]{2,1,0:T(8,128)(2,1)}), bf16[2,1024,4096]{2,1,0:T(8,128)(2,1)}) %all-gather.2.cloned.1.call-update) | async-done | bytes 16777232 | tf_op jit(solution)/shard_map/all_gather | solution.py:56
  162.1 22.0 %fusion.26 = bf16[2048,772]{0,1:T(8,128)(2,1)} fusion(bf16[2048,4096]{1,0:T(8,128)(2,1)} %bitcast.87, bf16[4096,4]{1,0:T(8,128)(2,1)S(1)} %copy.23, bf16[4096,256]{1,0:T(8,128)(2,1)} %param.17, bf16[4096,256]{1,0:T(8,128)(2,1)} %param.16, bf16[4096,256]{1,0:T(8,128)(2,1)} %param.15), kind=kOutput, calls=%fused_computation.32 | convolution fusion | flops 12978888704 | bytes 26263552 | tf_op jit(solution)/shard_map/dot_general | solution.py:57
  184.2 8.8 %reshape.152 = bf16[2,1024,772]{1,0,2:T(2,128)(2,1)} reshape(bf16[2048,772]{0,1:T(8,128)(2,1)} %fusion.26) | data formatting | bytes 6324224 | tf_op jit(solution)/shard_map/reshape | solution.py:58
  193.0 3.3 slice_convert_fusion
  196.3 4.4 slice.97
  202.9 2.3 reduce-window.6
  207.4 6.2 %copy.36 = bf16[2,1024,512]{2,1,0:T(8,128)(2,1)} copy(bf16[2,1024,512]{1,0,2:T(2,128)(2,1)} %slice.97) | data formatting | bytes 4194304
  213.7 1.7 collective-permute-start
  215.4 3.8 copy.39
  220.6 5.4 %collective-permute-done.2 = bf16[2,4]{1,0:T(2,128)(2,1)S(1)} collective-permute-done((bf16[2,4]{1,0:T(2,128)(2,1)S(1)}, bf16[2,4]{1,0:T(2,128)(2,1)S(1)}, u32[]{:S(2)}, u32[]{:S(2)}) %collective-permute-start.2) | collective-permute-done | bytes 48 | tf_op jit(solution)/shard_map/ppermute | solution.py:12
  228.0 2.5 divide_multiply_fusion
  230.5 2.0 copy-done.1
  234.0 2.9 copy.27
  236.9 4.0 add_convert_fusion.2
  242.2 7.1 %collective-permute-done.4 = bf16[2,4,64,128]{3,2,1,0:T(8,128)(2,1)S(1)} collective-permute-done((bf16[2,4,64,128]{3,2,1,0:T(8,128)(2,1)S(1)}, bf16[2,4,64,128]{3,2,1,0:T(8,128)(2,1)S(1)}, u32[]{:S(2)}, u32[]{:S(2)}) %collective-permute-start.4) | collective-permute-done | bytes 131104 | tf_op jit(solution)/shard_map/ppermute | solution.py:12
  250.9 10.6 %fusion.43 = f32[2,1024,1024]{2,1,0:T(8,128)} fusion(f32[2,1024,512]{2,1,0:T(8,128)} %copy-done.1), kind=kOutput, calls=%fused_computation.52 | convolution fusion | flops 3221225472 | bytes 10485760 | tf_op jit(solution)/shard_map/bin,bjn->bij/dot_general | solution.py:81
  262.9 50.2 %fusion = f32[2,4,64,1024]{3,2,1,0:T(8,128)} fusion(f32[2,1024,1024]{2,1,0:T(8,128)} %fusion.43, f32[1024,1024]{1,0:T(8,128)S(1)} %copy-done.4, f32[2,4,1024]{2,1,0:T(4,128)S(1)} %reduce_window_sum.24, f32[2,1024,4,64]{1,3,2,0:T(8,128)S(1)} %bitcast.75, f32[2,1024,4]{1,2,0:T(4,128)S(1)} %copy.24), kind=kOutput, calls=%fused_computation.1 | convolution fusion | flops 6476529664 | bytes 16842752 | tf_op jit(solution)/shard_map/bhij,bjhp->bihp/dot_general | solution.py:86
  313.1 5.4 %multiply_reduce_fusion = (f32[2,1024]{1,0:T(2,128)S(1)}, f32[2,1024,4,64]{1,3,2,0:T(8,128)S(1)}) fusion(f32[2,1024,256]{1,0,2:T(2,128)} %slice_convert_fusion, f32[2,1024]{1,0:T(2,128)S(1)} %compare_convert_fusion, f32[2,1024,4]{1,2,0:T(4,128)S(1)} %get-tuple-element.12, bf16[2,4,64,128]{3,2,1,0:T(8,128)(2,1)S(1)} %collective-permute-done.6, ...), kind=kOutput, calls=%fused_computation.37 | convolution fusion | flops 811005952 | bytes 7651360 | tf_op jit(solution)/shard_map/bhpn,bin->bihp/dot_general | solution.py:112
  320.1 2.2 copy.38
  322.3 13.9 %psum.23 = f32[2048]{0:T(1024)S(1)} all-reduce(f32[2048]{0:T(1024)S(1)} %bitcast.79), channel_id=1, replica_groups=mesh['seq'=4,'head'=8] {'head'}, use_global_device_ids=true, to_apply=%region_5.6 | all-reduce | flops 2048 | bytes 16384 | tf_op jit(solution)/shard_map/psum | solution.py:117
  336.3 11.3 %convert_bitcast_fusion = bf16[4096,2048]{0,1:T(8,128)(2,1)} fusion(bf16[256,4096]{1,0:T(8,128)(2,1)S(1)} %copy-done, f32[2048,256]{0,1:T(8,128)} %bitcast.78, f32[2048,256]{0,1:T(8,128)} %bitcast.77, f32[256]{0:T(256)S(1)} %copy-done.11, f32[2048]{0:T(1024)S(1)} %add_rsqrt_fusion), kind=kOutput, calls=%fused_computation.7 | convolution fusion | flops 4307550208 | bytes 23077888 | tf_op jit(solution)/shard_map/dot_general | solution.py:121
  347.6 170.6 %reduce-scatter.2.cloned.1.call-done = bf16[512,2048]{0,1:T(8,128)(2,1)} async-done(((bf16[4096,2048]{0,1:T(8,128)(2,1)}), bf16[512,2048]{0,1:T(8,128)(2,1)}) %reduce-scatter.2.cloned.1.call-update) | async-done | bytes 2097168 | tf_op jit(solution)/shard_map/reduce_scatter | solution.py:120
  (75 shorter events, 18.7 us)
Async XLA Ops:
  7.4 328.9 %copy-start = (bf16[256,4096]{1,0:T(8,128)(2,1)S(1)}, bf16[256,4096]{1,0:T(8,128)(2,1)}, u32[]{:S(2)}) copy-start(bf16[256,4096]{1,0:T(8,128)(2,1)} %param.24) | copy-start | bytes 6291460
  7.4 8.2 %copy-start.5 = (bf16[4096,4]{0,1:T(4,128)(2,1)S(1)}, bf16[4096,4]{0,1:T(4,128)(2,1)}, u32[]{:S(2)}) copy-start(bf16[4096,4]{0,1:T(4,128)(2,1)} %param.18) | copy-start | bytes 98308
  7.4 154.7 %all-gather.2.cloned.1.call-start = ((), (), s32[]{:S(2)}) async-start(), calls=%async_computation.1 | async-start | bytes 18874368 | tf_op jit(solution)/shard_map/all_gather | solution.py:56
  8.1 8.0 %copy-start.6 = (f32[4,256]{1,0:T(4,128)S(1)}, f32[4,256]{1,0:T(4,128)}, u32[]{:S(2)}) copy-start(f32[4,256]{1,0:T(4,128)} %param.21) | copy-start | bytes 12292
  8.1 8.1 %copy-start.7 = (f32[4,256]{1,0:T(4,128)S(1)}, f32[4,256]{1,0:T(4,128)}, u32[]{:S(2)}) copy-start(f32[4,256]{1,0:T(4,128)} %param.22) | copy-start | bytes 12292
  8.1 8.1 %copy-start.10 = (s32[2]{0:T(128)S(1)}, s32[2]{0:T(128)}, u32[]{:S(2)}) copy-start(s32[2]{0:T(128)} %param.27) | copy-start | bytes 28
  8.1 305.0 %all-reduce.3.cloned.1.call-start = ((), (), s32[]{:S(2)}) async-start(), calls=%async_computation.3 | async-start | bytes 262144 | tf_op jit(solution)/shard_map/psum | solution.py:25
  13.1 505.1 %reduce-scatter.2.cloned.1.call-start = ((), (), s32[]{:S(2)}) async-start(), calls=%async_computation.2 | async-start | bytes 18874368 | tf_op jit(solution)/shard_map/reduce_scatter | solution.py:120
  193.0 9.0 %copy-start.8 = (f32[4]{0:T(128)S(1)}, f32[4]{0:T(128)}, u32[]{:S(2)}) copy-start(f32[4]{0:T(128)} %param.20) | copy-start | bytes 52
  193.0 9.0 %copy-start.9 = (f32[4]{0:T(128)S(1)}, f32[4]{0:T(128)}, u32[]{:S(2)}) copy-start(f32[4]{0:T(128)} %param.19) | copy-start | bytes 52
  206.1 13.2 %collective-permute-start.1 = (bf16[2,4]{1,0:T(2,128)(2,1)S(1)}, bf16[2,4]{1,0:T(2,128)(2,1)S(1)}, u32[]{:S(2)}, u32[]{:S(2)}) collective-permute-start(bf16[2,4]{1,0:T(2,128)(2,1)S(1)} %fusion.60), channel_id=1, source_target_pairs={{0,8},{8,16},{16,24},{1,9},{9,17},{17,25},{2,10},{10,18},{18,26},{... | collective-permute-start | bytes 56 | tf_op jit(solution)/shard_map/ppermute | solution.py:12
  213.7 13.6 %copy-start.3 = (bf16[2,1024,512]{2,1,0:T(8,128)(2,1)S(1)}, bf16[2,1024,512]{2,1,0:T(8,128)(2,1)}, u32[]{:S(2)}) copy-start(bf16[2,1024,512]{2,1,0:T(8,128)(2,1)} %copy.36) | copy-start | bytes 6291460
  213.7 13.6 %collective-permute-start = (bf16[2,3,512]{2,1,0:T(4,128)(2,1)S(1)}, bf16[2,3,512]{2,1,0:T(4,128)(2,1)S(1)}, u32[]{:S(2)}, u32[]{:S(2)}) collective-permute-start(bf16[2,3,512]{2,1,0:T(4,128)(2,1)S(1)} %copy.35), channel_id=1, source_target_pairs={{0,8},{8,16},{16,24},{1,9},{9,17},{17,25},{2,10},{10,18},{18,26},{... | collective-permute-start | bytes 18440 | tf_op jit(solution)/shard_map/ppermute | solution.py:12
  219.3 6.7 %collective-permute-start.2 = (bf16[2,4]{1,0:T(2,128)(2,1)S(1)}, bf16[2,4]{1,0:T(2,128)(2,1)S(1)}, u32[]{:S(2)}, u32[]{:S(2)}) collective-permute-start(bf16[2,4]{1,0:T(2,128)(2,1)S(1)} %multiply_convert_fusion.3), channel_id=1, source_target_pairs={{0,8},{8,16},{16,24},{1,9},{9,17},{17,25},{2,10},{10,18},{18,26},{... | collective-permute-start | bytes 56 | tf_op jit(solution)/shard_map/ppermute | solution.py:12
  226.0 16.2 %collective-permute-start.3 = (bf16[2,4]{1,0:T(2,128)(2,1)S(1)}, bf16[2,4]{1,0:T(2,128)(2,1)S(1)}, u32[]{:S(2)}, u32[]{:S(2)}) collective-permute-start(bf16[2,4]{1,0:T(2,128)(2,1)S(1)} %get-tuple-element.17), channel_id=1, source_target_pairs={{0,8},{8,16},{16,24},{1,9},{9,17},{17,25},{2,10},{10,18},{18,26},{... | collective-permute-start | bytes 56 | tf_op jit(solution)/shard_map/ppermute | solution.py:12
  230.5 2.0 copy-start.1
  240.8 8.4 %collective-permute-start.4 = (bf16[2,4,64,128]{3,2,1,0:T(8,128)(2,1)S(1)}, bf16[2,4,64,128]{3,2,1,0:T(8,128)(2,1)S(1)}, u32[]{:S(2)}, u32[]{:S(2)}) collective-permute-start(bf16[2,4,64,128]{3,2,1,0:T(8,128)(2,1)S(1)} %get-tuple-element.24), channel_id=1, source_target_pairs={{0,8},{8,16},{16,24},{1,9},{9,17},{17,25},{2,10},{10,18},{18,26},{... | collective-permute-start | bytes 393224 | tf_op jit(solution)/shard_map/ppermute | solution.py:12
  249.3 13.6 %copy-start.2 = (f32[2,1024,256]{1,2,0:T(8,128)S(1)}, f32[2,1024,256]{1,2,0:T(8,128)}, u32[]{:S(2)}) copy-start(f32[2,1024,256]{1,2,0:T(8,128)} %copy.27) | copy-start | bytes 6291460
  249.4 13.6 %copy-start.4 = (f32[1024,1024]{1,0:T(8,128)S(1)}, f32[1024,1024]{1,0:T(8,128)}, u32[]{:S(2)}) copy-start(f32[1024,1024]{1,0:T(8,128)} %fusion.22) | copy-start | bytes 12582916
  249.4 12.1 %collective-permute-start.5 = (bf16[2,4,64,128]{3,2,1,0:T(8,128)(2,1)S(1)}, bf16[2,4,64,128]{3,2,1,0:T(8,128)(2,1)S(1)}, u32[]{:S(2)}, u32[]{:S(2)}) collective-permute-start(bf16[2,4,64,128]{3,2,1,0:T(8,128)(2,1)S(1)} %add_convert_fusion.1), channel_id=1, source_target_pairs={{0,8},{8,16},{16,24},{1,9},{9,17},{17,25},{2,10},{10,18},{18,26},{... | collective-permute-start | bytes 393224 | tf_op jit(solution)/shard_map/ppermute | solution.py:12
  261.6 51.5 %collective-permute-start.6 = (bf16[2,4,64,128]{3,2,1,0:T(8,128)(2,1)S(1)}, bf16[2,4,64,128]{3,2,1,0:T(8,128)(2,1)S(1)}, u32[]{:S(2)}, u32[]{:S(2)}) collective-permute-start(bf16[2,4,64,128]{3,2,1,0:T(8,128)(2,1)S(1)} %add_convert_fusion), channel_id=1, source_target_pairs={{0,8},{8,16},{16,24},{1,9},{9,17},{17,25},{2,10},{10,18},{18,26},{... | collective-permute-start | bytes 393224 | tf_op jit(solution)/shard_map/ppermute | solution.py:12
  318.5 17.8 %copy-start.11 = (f32[256]{0:T(256)S(1)}, f32[256]{0:T(256)}, u32[]{:S(2)}) copy-start(f32[256]{0:T(256)} %param.23) | copy-start | bytes 3076
Sparse Core Ops, SparseCore 0:
  9.8 152.2 all-gather.1
  347.8 170.4 reduce-scatter.1
Sparse Core Ops, SparseCore 1:
  13.2 41.9 all-reduce.2
where the time goes:
time: 533 us; the launch traced here: 526 us
  waiting for transfers between devices  330 us (62%)
  matrix products  103 us (19%)
  local copies, waits for them, and re-layouts  38.2 us (7%)
  between operations  16.7 us (3%)
  other arithmetic  14.2 us (3%)
  blocking collectives  13.9 us (3%)
  starting transfers between devices  9.78 us (2%)
    reduce_scatter x1, waiting for transfers between devices, per_device(): lax.psum_scatter(lax.dot_general(w_out, normed, (((0,), (1,)), ((), ())),...  171 us
    all_gather x1, waiting for transfers between devices, per_device(): piece = lax.all_gather(tokens, 'head', axis=2, tiled=True)  146 us
    dot_general x1, matrix products, per_device(): y_local = jnp.einsum('bhij,bjhp->bihp', weighting, drive, precision=high)  50.2 us
    dot_general x1, matrix products, per_device(): jnp.dot(piece.reshape(-1, piece.shape[2]), weights, preferred_element_typ...  22 us
    unnamed x32, local copies, waits for them, and re-layouts  15 us
    psum x1, blocking collectives, per_device(): squares = lax.psum(jnp.sum(gated * gated, axis=1), 'head')  13.9 us
    ppermute x7, waiting for transfers between devices, passed_along(): return lax.ppermute(block, axis, route)  12.5 us
    dot_general x1, matrix products, per_device(): lax.dot_general(w_out, normed, (((0,), (1,)), ((), ())), preferred_elemen...  11.3 us
  transfers between devices with their start and end apart: 10, of which 4 were waited for; matrix products, arithmetic and copies ran while one was open for 25% of the time, Pallas kernels for 0%

commit v1 on v0

v1 whole, which is shorter than its diff:
```python
import functools

import jax
import jax.numpy as jnp
from jax import lax
from jax.experimental import pallas as pl
from jax.experimental.pallas import tpu as pltpu
from jax.sharding import PartitionSpec as P

CONV = 4
LANES = 128
CHUNK = 128
F32 = jnp.float32
BF16 = jnp.bfloat16


def silu(x):
    return x * (1.0 / (1.0 + jnp.exp(-x)))


def softplus(x):
    return jnp.maximum(x, 0.0) + jnp.log1p(jnp.exp(-jnp.abs(x)))


def per_head(cols, heads, size):
    rows = cols.shape[0]
    return jnp.concatenate(
        [jnp.broadcast_to(cols[:, h : h + 1], (rows, size)) for h in range(heads)], axis=1
    )


def scan_kernel(
    heads, inner, state, mixin_ref, step_ref, before_ref, taps_ref, bias_ref, rate_ref, start_ref,
    y_ref, c_ref, grow_ref, sec_ref, total_ref, tail, held, passed,
):
    i = pl.program_id(0)
    rows = mixin_ref.shape[0]
    size = inner // heads

    @pl.when(i == 0)
    def _():
        tail[...] = before_ref[...].astype(F32)
        held[...] = jnp.zeros_like(held)
        passed[...] = jnp.zeros_like(passed)

    mixin = mixin_ref[...].astype(F32)
    padded = jnp.concatenate([tail[...], mixin], axis=0)
    tail[...] = mixin[rows - 8 :, :]
    conv = taps_ref[0:1, :] * padded[8 - CONV + 1 : 8 - CONV + 1 + rows, :]
    for k in range(1, CONV):
        conv = conv + taps_ref[k : k + 1, :] * padded[8 - CONV + 1 + k : 8 - CONV + 1 + k + rows, :]
    conv = silu(conv)
    xs = conv[:, :inner]
    bmat = conv[:, inner : inner + state].astype(BF16)
    cmat = conv[:, inner + state :].astype(BF16)
    c_ref[...] = cmat
    line = lax.broadcasted_iota(jnp.int32, (rows, LANES), 0)
    dt = softplus(step_ref[...].astype(F32) + bias_ref[...])
    dt = jnp.where(line + i * rows >= start_ref[0], dt, 0.0)
    tri_r = lax.broadcasted_iota(jnp.int32, (rows, rows), 0)
    tri_c = lax.broadcasted_iota(jnp.int32, (rows, rows), 1)
    lower = tri_r >= tri_c
    cumul = jnp.dot(
        lower.astype(F32), -dt * rate_ref[...],
        precision=lax.Precision.HIGHEST, preferred_element_type=F32,
    )
    cumul_t = cumul.T
    last = cumul[rows - 1 : rows, :]
    scores = lax.dot_general(cmat, bmat, (((1,), (1,)), ((), ())), preferred_element_type=F32)
    scores = jnp.where(lower, scores, 0.0)
    drive = per_head(dt, heads, size) * xs
    drive16 = drive.astype(BF16)
    from_held = lax.dot_general(
        cmat, held[...].astype(BF16), (((1,), (1,)), ((), ())), preferred_element_type=F32
    )
    within = jnp.exp(cumul)
    y = per_head(within, heads, size) * from_held
    parts = []
    for h in range(heads):
        diff = cumul[:, h : h + 1] - cumul_t[h : h + 1, :]
        weighting = (jnp.exp(jnp.minimum(diff, 0.0)) * scores).astype(BF16)
        parts.append(
            jnp.dot(weighting, drive16[:, h * size : (h + 1) * size], preferred_element_type=F32)
        )
    y_ref[...] = y + jnp.concatenate(parts, axis=1)
    to_end = per_head(jnp.exp(last - cumul), heads, size)
    added = lax.dot_general(
        (to_end * drive).astype(BF16), bmat, (((0,), (0,)), ((), ())), preferred_element_type=F32
    )
    for h in range(heads):
        keep = jnp.exp(last[:, h : h + 1])
        at = slice(h * size, (h + 1) * size)
        held[at, :] = keep * held[at, :] + added[at, :]
    grow_ref[...] = jnp.exp(cumul + passed[0:1, :])
    passed[...] = passed[...] + last
    sec_ref[...] = held[...]
    total_ref[...] = jnp.exp(passed[...])


def scan_section(proj, before, taps, bias, rate, start, heads, inner, state):
    length = proj.shape[0]
    mix = inner + 2 * state
    step_at = (mix + inner) // LANES
    whole = lambda shape: pl.BlockSpec(shape, lambda i: (0,) * len(shape))
    return pl.pallas_call(
        functools.partial(scan_kernel, heads, inner, state),
        grid=(length // CHUNK,),
        in_specs=[
            pl.BlockSpec((CHUNK, mix), lambda i: (i, 0)),
            pl.BlockSpec((CHUNK, LANES), lambda i: (i, step_at)),
            whole((8, mix)),
            whole((CONV, mix)),
            whole((1, LANES)),
            whole((1, LANES)),
            pl.BlockSpec(memory_space=pltpu.SMEM),
        ],
        out_specs=[
            pl.BlockSpec((CHUNK, inner), lambda i: (i, 0)),
            pl.BlockSpec((CHUNK, state), lambda i: (i, 0)),
            pl.BlockSpec((CHUNK, LANES), lambda i: (i, 0)),
            whole((inner, state)),
            whole((8, LANES)),
        ],
        out_shape=[
            jax.ShapeDtypeStruct((length, inner), F32),
            jax.ShapeDtypeStruct((length, state), BF16),
            jax.ShapeDtypeStruct((length, LANES), F32),
            jax.ShapeDtypeStruct((inner, state), F32),
            jax.ShapeDtypeStruct((8, LANES), F32),
        ],
        scratch_shapes=[
            pltpu.VMEM((8, mix), F32),
            pltpu.VMEM((inner, state), F32),
            pltpu.VMEM((8, LANES), F32),
        ],
        cost_estimate=pl.CostEstimate(
            flops=2 * length * inner * 4 * LANES, bytes_accessed=length * 4096,
            transcendentals=length * 2048,
        ),
        name="section_scan",
    )(proj, proj, before, taps, bias, rate, start)


def gate_kernel(heads, y_ref, c_ref, grow_ref, gate_ref, inc_ref, gain_ref, start_ref, g_ref, sq_ref):
    i = pl.program_id(0)
    rows, inner = y_ref.shape
    carry = lax.dot_general(
        c_ref[...], inc_ref[...], (((1,), (1,)), ((), ())), preferred_element_type=F32
    )
    y = y_ref[...] + per_head(grow_ref[...], heads, inner // heads) * carry
    line = lax.broadcasted_iota(jnp.int32, (rows, inner), 0)
    y = jnp.where(line + i * rows >= start_ref[0], y, 0.0)
    gated = y * silu(gate_ref[...].astype(F32))
    sq_ref[...] = jnp.broadcast_to(jnp.sum(gated * gated, axis=1, keepdims=True), sq_ref.shape)
    g_ref[...] = (gated * gain_ref[...]).astype(BF16)


def gate_section(y, cmat, grow, proj, incoming, gain, start, heads, mix):
    length, inner = y.shape
    state = cmat.shape[1]
    rows = 256
    at = mix // inner
    return pl.pallas_call(
        functools.partial(gate_kernel, heads),
        grid=(length // rows,),
        in_specs=[
            pl.BlockSpec((rows, inner), lambda i: (i, 0)),
            pl.BlockSpec((rows, state), lambda i: (i, 0)),
            pl.BlockSpec((rows, LANES), lambda i: (i, 0)),
            pl.BlockSpec((rows, inner), lambda i: (i, at)),
            pl.BlockSpec((inner, state), lambda i: (0, 0)),
            pl.BlockSpec((1, inner), lambda i: (0, 0)),
            pl.BlockSpec(memory_space=pltpu.SMEM),
        ],
        out_specs=[
            pl.BlockSpec((rows, inner), lambda i: (i, 0)),
            pl.BlockSpec((rows, LANES), lambda i: (i, 0)),
        ],
        out_shape=[
            jax.ShapeDtypeStruct((length, inner), BF16),
            jax.ShapeDtypeStruct((length, LANES), F32),
        ],
        cost_estimate=pl.CostEstimate(
            flops=2 * length * inner * LANES, bytes_accessed=length * 3000,
            transcendentals=length * inner,
        ),
        name="section_gate",
    )(y, cmat, grow, proj, incoming, gain, start)


def high_low(x):
    high = x.astype(BF16)
    return high, (x - high.astype(F32)).astype(BF16)


def per_device(
    tokens, w_gate, w_value, w_bc, w_step, step_bias, rate, conv_value, conv_bc, norm_gain,
    w_out, kept_states, kept_index, cached_len,
):
    batch, sec_len, d_part = tokens.shape
    inner = w_gate.shape[1]
    heads = w_step.shape[1]
    size = inner // heads
    state = w_bc.shape[1] // 2
    mix = inner + 2 * state
    slots = kept_states.shape[0]
    n_seq = lax.axis_size("seq")
    n_head = lax.axis_size("head")
    sec = lax.axis_index("seq")

    pieces = [lax.all_gather(tokens[b], "head", axis=1, tiled=True) for b in range(batch)]
    w_cols = lax.all_to_all(w_out, "head", split_axis=1, concat_axis=0, tiled=True)
    weights = jnp.concatenate(
        [w_value, w_bc, w_gate, jnp.pad(w_step, ((0, 0), (0, LANES - heads)))], axis=1
    )
    taps = jnp.concatenate([conv_value, conv_bc], axis=1)
    bias = jnp.pad(step_bias, (0, LANES - heads))[None]
    rates = jnp.pad(rate, (0, LANES - heads))[None]
    gain = norm_gain[None]
    picked = jnp.stack(
        [lax.dynamic_index_in_dim(kept_states, kept_index[b] % slots, 0, False) for b in range(batch)]
    ).astype(BF16).reshape(batch, inner, state)
    kept = lax.all_gather(picked, "seq", axis=0)

    outs = []
    for b in range(batch):
        proj = jnp.dot(pieces[b], weights, preferred_element_type=F32).astype(BF16)
        before = lax.ppermute(
            proj[sec_len - 8 :, :mix], "seq", [(i, i + 1) for i in range(n_seq - 1)]
        )
        start = (cached_len[b] - sec * sec_len)[None]
        y, cmat, grow, sec_state, total = scan_section(
            proj, before, taps, bias, rates, start, heads, inner, state
        )
        high, low = high_low(total)
        sent = jnp.concatenate([sec_state.astype(BF16), high, low], axis=0)
        got = lax.all_gather(sent, "seq", axis=0)
        incoming = lax.dynamic_index_in_dim(kept, kept_index[b] // slots, 0, False)[b]
        incoming = incoming.astype(F32).reshape(heads, size, state)
        for r in range(n_seq - 1):
            decay = got[r, inner, :heads].astype(F32) + got[r, inner + 8, :heads].astype(F32)
            later = decay[:, None, None] * incoming + got[r, :inner].astype(F32).reshape(
                heads, size, state
            )
            incoming = jnp.where(r < sec, later, incoming)
        g, squares = gate_section(
            y, cmat, grow, proj, incoming.reshape(inner, state).astype(BF16), gain, start, heads, mix
        )
        g_all = lax.all_gather(g, "head", axis=1, tiled=True)
        sq_all = lax.all_gather(squares[:, 0], "head", axis=0)
        meansq = jnp.sum(sq_all, axis=0) / (inner * n_head)
        mixed = jnp.dot(g_all, w_cols, preferred_element_type=F32)
        outs.append((mixed * lax.rsqrt(meansq + 1e-05)[:, None]).astype(BF16))
    return jnp.stack(outs)


def solution(mesh):
    return jax.shard_map(
        per_device,
        mesh=mesh,
        in_specs=(
            P(None, "seq", "head"),
            P(None, "head"),
            P(None, "head"),
            P(),
            P(None, "head"),
            P("head"),
            P("head"),
            P(None, "head"),
            P(),
            P("head"),
            P("head", None),
            P("seq", "head", None, None),
            P(),
            P(),
        ),
        out_specs=P(None, "seq", "head"),
        check_vma=False,
    )
```

time: 533 us -> 470 us (0.88)
  blocking collectives: 13.9 us -> 222 us
  waiting for transfers between devices: 330 us -> 131 us
  matrix products: 103 us -> 37 us
  Pallas kernels: 0 us -> 27.3 us
  local copies, waits for them, and re-layouts: 38.2 us -> 14.7 us
  starting transfers between devices: 9.78 us -> 2.91 us
    reduce_scatter x1 -> x0, waiting for transfers between devices: 171 us -> none  [per_device(): lax.psum_scatter(lax.dot_general(w_out, normed, (((0,), (1,)), ((), ())),...]
    all_gather x0 -> x5, blocking collectives: none -> 140 us  [the longest x2 112 us: per_device(): sq_all = lax.all_gather(squares[:, 0], 'head', axis=0)]
    all_to_all x0 -> x1, blocking collectives: none -> 82.2 us  [per_device(): lax.all_to_all(w_out, 'head', split_axis=1, concat_axis=0, tiled=True)]
    dot_general x6 -> x4, matrix products: 103 us -> 37 us  [the longest x2 28 us: per_device(): proj = jnp.dot(pieces[b], weights, preferred_element_type=F32).astype(BF16)]
    pallas_call x0 -> x4, Pallas kernels: none -> 27.3 us  [the longest x2 18.5 us: scan_section(): pl.pallas_call(functools.partial(scan_kernel, heads, inner, state), grid=...]
    all_gather x1 -> x4, waiting for transfers between devices: 146 us -> 131 us  [the longest x2 131 us: per_device(): lax.all_gather(tokens[b], 'head', axis=1, tiled=True)]
    psum x1 -> x0, blocking collectives: 13.9 us -> none  [per_device(): squares = lax.psum(jnp.sum(gated * gated, axis=1), 'head')]
    ppermute x7 -> x2, waiting for transfers between devices: 12.5 us -> 0.01 us  [per_device(): lax.ppermute(proj[sec_len - 8:, :mix], 'seq', [(i, i + 1) for i in range(...]
  transfers between devices with their start and end apart: 10 -> 6, of which waited for: 4 -> 2; matrix products, arithmetic and copies ran while one was open for 25% -> 11% of each run, Pallas kernels for 0% -> 3%
where the time goes in v1:
time: 470 us; the launch traced here: 468 us
  blocking collectives  222 us (47%)
  waiting for transfers between devices  131 us (28%)
  matrix products  37 us (8%)
  Pallas kernels  27.3 us (6%)
  between operations  19.7 us (4%)
  local copies, waits for them, and re-layouts  14.7 us (3%)
  other arithmetic  12.5 us (3%)
    all_gather x2, waiting for transfers between devices, per_device(): lax.all_gather(tokens[b], 'head', axis=1, tiled=True)  131 us
    all_gather x2, blocking collectives, per_device(): sq_all = lax.all_gather(squares[:, 0], 'head', axis=0)  112 us
    all_to_all x1, blocking collectives, per_device(): lax.all_to_all(w_out, 'head', split_axis=1, concat_axis=0, tiled=True)  82.2 us
    dot_general x2, matrix products, per_device(): proj = jnp.dot(pieces[b], weights, preferred_element_type=F32).astype(BF16)  28 us
    all_gather x2, blocking collectives, per_device(): got = lax.all_gather(sent, 'seq', axis=0)  18.6 us
    pallas_call x2, Pallas kernels, scan_section(): pl.pallas_call(functools.partial(scan_kernel, heads, inner, state), grid=...  18.5 us
  transfers between devices with their start and end apart: 6, of which 2 were waited for; matrix products, arithmetic and copies ran while one was open for 11% of the time, Pallas kernels for 3%

profile of v1, /device:TPU:6, one launch (start us, length us, event | category | flops | bytes accessed | tf_op | source)
XLA Modules:
  0.0 467.6 jit_solution(16352047778876505906)
XLA Ops:
  6.6 3.0 fusion.34
  19.6 9.1 %all_gather.36 = bf16[4,2,256,128]{3,2,1,0:T(8,128)(2,1)S(1)} all-gather(bf16[1,2,256,128]{3,2,1,0:T(8,128)(2,1)S(1)} %pad_maximum_fusion.1), channel_id=1, replica_groups=mesh['seq'=4,'head'=8] {'seq'}, dimensions={0}, use_global_device_ids=true | all-gather | bytes 655360 | tf_op jit(solution)/shard_map/all_gather | solution.py:223
  29.3 63.7 %all-gather.15.cloned.1.call-done = bf16[1,1024,4096]{2,1,0:T(8,128)(2,1)} async-done(((bf16[1,1024,512]{2,1,0:T(8,128)(2,1)}), bf16[1,1024,4096]{2,1,0:T(8,128)(2,1)}) %all-gather.15.cloned.1.call-update) | async-done | bytes 8388624 | tf_op jit(solution)/shard_map/all_gather | solution.py:211
  93.1 14.0 %convert_bitcast_fusion.1.mixin_ref.step_ref.gate_ref = bf16[1024,896]{1,0:T(8,128)(2,1)S(1)} fusion(bf16[1,1024,4096]{2,1,0:T(8,128)(2,1)} %all-gather.15.cloned.1.call-done, bf16[4096,4]{1,0:T(8,128)(2,1)S(1)} %copy.33, bf16[4096,256]{1,0:T(8,128)(2,1)} %param.15, bf16[4096,256]{1,0:T(8,128)(2,1)} %param.17, bf16[4096,256]{1,0:T(8,128)(2,1)} %param.16), kind=kOutput, calls=%fused_computation.11 | convolution fusion | flops 7553810432 | bytes 16547840 | tf_op jit(solution)/shard_map/dot_general | solution.py:227
  107.1 1.3 collective-permute-start
  108.4 66.9 %all-gather.17.cloned.1.call-done = bf16[1,1024,4096]{2,1,0:T(8,128)(2,1)} async-done(((bf16[1,1024,512]{2,1,0:T(8,128)(2,1)}), bf16[1,1024,4096]{2,1,0:T(8,128)(2,1)}) %all-gather.17.cloned.1.call-update) | async-done | bytes 8388624 | tf_op jit(solution)/shard_map/all_gather | solution.py:211
  175.3 14.0 %convert_bitcast_fusion.mixin_ref.step_ref.gate_ref = bf16[1024,896]{1,0:T(8,128)(2,1)S(1)} fusion(bf16[1,1024,4096]{2,1,0:T(8,128)(2,1)} %all-gather.17.cloned.1.call-done, bf16[4096,4]{1,0:T(8,128)(2,1)S(1)} %copy.33, bf16[4096,256]{1,0:T(8,128)(2,1)} %param.15, bf16[4096,256]{1,0:T(8,128)(2,1)} %param.17, bf16[4096,256]{1,0:T(8,128)(2,1)} %param.16), kind=kOutput, calls=%fused_computation.10 | convolution fusion | flops 7553810432 | bytes 16547840 | tf_op jit(solution)/shard_map/dot_general | solution.py:227
  190.5 1.5 collective-permute-start.1
  192.6 9.3 %section_scan.2 = (f32[1024,256]{1,0:T(8,128)}, bf16[1024,128]{1,0:T(8,128)(2,1)}, f32[1024,128]{1,0:T(8,128)}, f32[256,128]{1,0:T(8,128)}, f32[8,128]{1,0:T(8,128)}) custom-call(bf16[1024,896]{1,0:T(8,128)(2,1)} %copy-done.2, bf16[1024,896]{1,0:T(8,128)(2,1)} %copy-done.2, bf16[8,512]{1,0:T(8,128)(2,1)} %copy-done.15, f32[4,512]{1,0:T(4,128)} %copy-done.9, ...), custom_call_target="tpu_custom_call" | custom-call | flops 268435456 | bytes 4194304 | tf_op jit(solution)/shard_map/section_scan/pallas_call | solution.py:105
  203.5 10.3 %all-gather.1 = bf16[1088,128]{1,0:T(8,128)(2,1)S(1)} all-gather(bf16[272,128]{1,0:T(8,128)(2,1)S(1)} %pad_maximum_fusion.2), channel_id=3, replica_groups=mesh['seq'=4,'head'=8] {'seq'}, dimensions={0}, use_global_device_ids=true | all-gather | bytes 348160 | tf_op jit(solution)/shard_map/all_gather | solution.py:237
  214.9 9.3 %section_scan.3 = (f32[1024,256]{1,0:T(8,128)}, bf16[1024,128]{1,0:T(8,128)(2,1)}, f32[1024,128]{1,0:T(8,128)}, f32[256,128]{1,0:T(8,128)}, f32[8,128]{1,0:T(8,128)}) custom-call(bf16[1024,896]{1,0:T(8,128)(2,1)} %copy-done.3, bf16[1024,896]{1,0:T(8,128)(2,1)} %copy-done.3, bf16[8,512]{1,0:T(8,128)(2,1)} %copy-done.14, f32[4,512]{1,0:T(4,128)} %copy-done.9, ...), custom_call_target="tpu_custom_call" | custom-call | flops 268435456 | bytes 4194304 | tf_op jit(solution)/shard_map/section_scan/pallas_call | solution.py:105
  225.8 8.4 %all-gather.4 = bf16[1088,128]{1,0:T(8,128)(2,1)S(1)} all-gather(bf16[272,128]{1,0:T(8,128)(2,1)S(1)} %pad_maximum_fusion.3), channel_id=6, replica_groups=mesh['seq'=4,'head'=8] {'seq'}, dimensions={0}, use_global_device_ids=true | all-gather | bytes 348160 | tf_op jit(solution)/shard_map/all_gather | solution.py:237
  235.6 4.4 section_gate.3
  240.2 4.3 section_gate.2
  244.5 2.5 copy.28
  247.0 82.2 %all_to_all.19 = bf16[256,8,512]{0,2,1:T(8,128)(2,1)S(1)} all-to-all(bf16[256,8,512]{0,2,1:T(8,128)(2,1)} %bitcast.95), channel_id=1, replica_groups=mesh['seq'=4,'head'=8] {'head'}, dimensions={1} | all-to-all | bytes 4194304 | tf_op jit(solution)/shard_map/all_to_all | solution.py:212
  329.1 2.4 copy.29
  331.5 72.3 %all-gather.5 = f32[8192,1]{1,0:T(8,128)} all-gather(f32[1024,1]{1,0:T(8,128)S(1)} %bitcast.102), channel_id=7, replica_groups=mesh['seq'=4,'head'=8] {'head'}, dimensions={0}, use_global_device_ids=true | all-gather | bytes 36864 | tf_op jit(solution)/shard_map/all_gather | solution.py:250
  403.8 3.3 reduce.1
  407.2 39.8 %all-gather.2 = f32[8192,1]{1,0:T(8,128)} all-gather(f32[1024,1]{1,0:T(8,128)S(1)} %bitcast.103), channel_id=4, replica_groups=mesh['seq'=4,'head'=8] {'head'}, dimensions={0}, use_global_device_ids=true | all-gather | bytes 36864 | tf_op jit(solution)/shard_map/all_gather | solution.py:250
  447.0 3.3 reduce
  450.5 4.5 fusion.11
  455.0 4.5 fusion.10
  459.6 1.5 pad_maximum_fusion
  (81 shorter events, 12.2 us)
Async XLA Ops:
  6.5 3.9 copy-start.10
  6.5 9.6 %copy-start.6 = (bf16[4096,4]{0,1:T(4,128)(2,1)S(1)}, bf16[4096,4]{0,1:T(4,128)(2,1)}, u32[]{:S(2)}) copy-start(bf16[4096,4]{0,1:T(4,128)(2,1)} %param.18) | copy-start | bytes 98308
  6.5 10.1 %copy-start.11 = (s32[2]{0:T(128)S(1)}, s32[2]{0:T(128)}, u32[]{:S(2)}) copy-start(s32[2]{0:T(128)} %param.27) | copy-start | bytes 28
  6.5 22.1 %copy-start.12 = (f32[4]{0:T(128)S(1)}, f32[4]{0:T(128)}, u32[]{:S(2)}) copy-start(f32[4]{0:T(128)} %param.20) | copy-start | bytes 52
  6.5 22.1 %copy-start.13 = (f32[4]{0:T(128)S(1)}, f32[4]{0:T(128)}, u32[]{:S(2)}) copy-start(f32[4]{0:T(128)} %param.19) | copy-start | bytes 52
  6.5 22.8 %copy-start.7 = (f32[4,256]{1,0:T(4,128)S(1)}, f32[4,256]{1,0:T(4,128)}, u32[]{:S(2)}) copy-start(f32[4,256]{1,0:T(4,128)} %param.21) | copy-start | bytes 12292
  6.6 22.7 %copy-start.8 = (f32[4,256]{1,0:T(4,128)S(1)}, f32[4,256]{1,0:T(4,128)}, u32[]{:S(2)}) copy-start(f32[4,256]{1,0:T(4,128)} %param.22) | copy-start | bytes 12292
  6.6 86.5 %all-gather.15.cloned.1.call-start = ((), (), s32[]{:S(2)}) async-start(), calls=%async_computation.3 | async-start | bytes 9437184 | tf_op jit(solution)/shard_map/all_gather | solution.py:211
  9.7 165.6 %all-gather.17.cloned.1.call-start = ((), (), s32[]{:S(2)}) async-start(), calls=%async_computation.4 | async-start | bytes 9437184 | tf_op jit(solution)/shard_map/all_gather | solution.py:211
  10.4 440.1 %all-gather.13.cloned.1.call-start = ((), (), s32[]{:S(2)}) async-start(), calls=%async_computation.2 | async-start | bytes 4718592 | tf_op jit(solution)/shard_map/all_gather | solution.py:249
  29.3 77.7 %copy-start.9 = (f32[4,512]{1,0:T(4,128)}, f32[4,512]{1,0:T(4,128)S(1)}, u32[]{:S(2)}) copy-start(f32[4,512]{1,0:T(4,128)S(1)} %constant_dynamic-update-slice_fusion.taps_ref) | copy-start | bytes 24580
  107.1 82.2 %copy-start.2 = (bf16[1024,896]{1,0:T(8,128)(2,1)}, bf16[1024,896]{1,0:T(8,128)(2,1)S(1)}, u32[]{:S(2)}) copy-start(bf16[1024,896]{1,0:T(8,128)(2,1)S(1)} %convert_bitcast_fusion.1.mixin_ref.step_ref.gate_ref) | copy-start | bytes 5505028
  107.1 84.9 %collective-permute-start = (bf16[8,512]{1,0:T(8,128)(2,1)S(1)}, bf16[8,512]{1,0:T(8,128)(2,1)S(1)}, u32[]{:S(2)}, u32[]{:S(2)}) collective-permute-start(bf16[8,512]{1,0:T(8,128)(2,1)S(1)} %slice.124), channel_id=1, source_target_pairs={{0,8},{8,16},{16,24},{1,9},{9,17},{17,25},{2,10},{10,18},{18,26},{... | collective-permute-start | bytes 24584 | tf_op jit(solution)/shard_map/ppermute | solution.py:228
  189.3 1.2 copy-start.3
  190.5 23.7 %collective-permute-start.1 = (bf16[8,512]{1,0:T(8,128)(2,1)S(1)}, bf16[8,512]{1,0:T(8,128)(2,1)S(1)}, u32[]{:S(2)}, u32[]{:S(2)}) collective-permute-start(bf16[8,512]{1,0:T(8,128)(2,1)S(1)} %slice.134), channel_id=1, source_target_pairs={{0,8},{8,16},{16,24},{1,9},{9,17},{17,25},{2,10},{10,18},{18,26},{... | collective-permute-start | bytes 24584 | tf_op jit(solution)/shard_map/ppermute | solution.py:228
  192.0 0.6 copy-start.15
  214.3 0.6 copy-start.14
  235.6 8.9 %copy-start = (bf16[256,4096]{1,0:T(8,128)(2,1)S(1)}, bf16[256,4096]{1,0:T(8,128)(2,1)}, u32[]{:S(2)}) copy-start(bf16[256,4096]{1,0:T(8,128)(2,1)} %param.24) | copy-start | bytes 6291460
  240.1 214.9 %all-gather.11.cloned.1.call-start = ((), (), s32[]{:S(2)}) async-start(), calls=%async_computation.1 | async-start | bytes 4718592 | tf_op jit(solution)/shard_map/all_gather | solution.py:249
  247.0 84.5 %copy-start.4 = (f32[1024,128]{1,0:T(8,128)S(1)}, f32[1024,128]{1,0:T(8,128)}, u32[]{:S(2)}) copy-start(f32[1024,128]{1,0:T(8,128)} %get-tuple-element.32) | copy-start | bytes 1572868
  331.5 75.7 %copy-start.5 = (f32[1024,128]{1,0:T(8,128)S(1)}, f32[1024,128]{1,0:T(8,128)}, u32[]{:S(2)}) copy-start(f32[1024,128]{1,0:T(8,128)} %get-tuple-element.25) | copy-start | bytes 1572868
  407.2 43.3 %copy-start.1 = (bf16[8,256,512]{2,1,0:T(8,128)(2,1)S(1)}, bf16[8,256,512]{2,1,0:T(8,128)(2,1)}, u32[]{:S(2)}) copy-start(bf16[8,256,512]{2,1,0:T(8,128)(2,1)} %copy.29) | copy-start | bytes 6291460
Sparse Core Ops, SparseCore 0:
  9.8 83.2 all-gather.14
  94.7 80.5 all-gather.16
  240.2 84.5 all-gather.12
  326.3 78.2 all-gather.10

commit v2 on v1

v2 whole, which is shorter than its diff:
```python
import functools

import jax
import jax.numpy as jnp
from jax import lax
from jax.experimental import pallas as pl
from jax.experimental.pallas import tpu as pltpu
from jax.sharding import PartitionSpec as P

CONV = 4
LANES = 128
CHUNK = 128
F32 = jnp.float32
BF16 = jnp.bfloat16


def silu(x):
    return x * (1.0 / (1.0 + jnp.exp(-x)))


def softplus(x):
    return jnp.maximum(x, 0.0) + jnp.log1p(jnp.exp(-jnp.abs(x)))


def per_head(cols, heads, size):
    rows = cols.shape[0]
    return jnp.concatenate(
        [jnp.broadcast_to(cols[:, h : h + 1], (rows, size)) for h in range(heads)], axis=1
    )


def scan_kernel(
    heads, inner, state, mixin_ref, step_ref, before_ref, taps_ref, bias_ref, rate_ref, start_ref,
    y_ref, c_ref, grow_ref, sec_ref, total_ref, tail, held, passed,
):
    i = pl.program_id(0)
    batch, rows = mixin_ref.shape[:2]
    size = inner // heads

    @pl.when(i == 0)
    def _():
        tail[...] = before_ref[...].astype(F32)
        held[...] = jnp.zeros_like(held)
        passed[...] = jnp.zeros_like(passed)

    tri_r = lax.broadcasted_iota(jnp.int32, (rows, rows), 0)
    tri_c = lax.broadcasted_iota(jnp.int32, (rows, rows), 1)
    lower = tri_r >= tri_c
    line = lax.broadcasted_iota(jnp.int32, (rows, LANES), 0) + i * rows
    for b in range(batch):
        mixin = mixin_ref[b].astype(F32)
        padded = jnp.concatenate([tail[b], mixin], axis=0)
        tail[b] = mixin[rows - 8 :, :]
        first = 8 - CONV + 1
        conv = taps_ref[0:1, :] * padded[first : first + rows, :]
        for k in range(1, CONV):
            conv = conv + taps_ref[k : k + 1, :] * padded[first + k : first + k + rows, :]
        conv = silu(conv)
        xs = conv[:, :inner]
        bmat = conv[:, inner : inner + state].astype(BF16)
        cmat = conv[:, inner + state :].astype(BF16)
        c_ref[b] = cmat
        dt = softplus(step_ref[b].astype(F32) + bias_ref[...])
        dt = jnp.where(line >= start_ref[b], dt, 0.0)
        cumul = jnp.dot(
            lower.astype(F32), -dt * rate_ref[...],
            precision=lax.Precision.HIGHEST, preferred_element_type=F32,
        )
        cumul_t = cumul.T
        last = cumul[rows - 1 : rows, :]
        scores = lax.dot_general(cmat, bmat, (((1,), (1,)), ((), ())), preferred_element_type=F32)
        scores = jnp.where(lower, scores, 0.0)
        drive = per_head(dt, heads, size) * xs
        drive16 = drive.astype(BF16)
        from_held = lax.dot_general(
            cmat, held[b].astype(BF16), (((1,), (1,)), ((), ())), preferred_element_type=F32
        )
        y = per_head(jnp.exp(cumul), heads, size) * from_held
        parts = []
        for h in range(heads):
            diff = cumul[:, h : h + 1] - cumul_t[h : h + 1, :]
            weighting = (jnp.exp(jnp.minimum(diff, 0.0)) * scores).astype(BF16)
            parts.append(
                jnp.dot(
                    weighting, drive16[:, h * size : (h + 1) * size], preferred_element_type=F32
                )
            )
        y_ref[b] = y + jnp.concatenate(parts, axis=1)
        to_end = per_head(jnp.exp(last - cumul), heads, size)
        added = lax.dot_general(
            (to_end * drive).astype(BF16), bmat, (((0,), (0,)), ((), ())),
            preferred_element_type=F32,
        )
        for h in range(heads):
            keep = jnp.exp(last[:, h : h + 1])
            at = slice(h * size, (h + 1) * size)
            held[b, at, :] = keep * held[b, at, :] + added[at, :]
        grow_ref[b] = jnp.exp(cumul + passed[b, 0:1, :])
        passed[b] = passed[b] + last
    sec_ref[...] = held[...]
    total_ref[...] = jnp.exp(passed[...])


def scan_section(proj, before, taps, bias, rate, start, heads, inner, state):
    batch, length = proj.shape[:2]
    mix = inner + 2 * state
    step_at = (mix + inner) // LANES
    whole = lambda shape: pl.BlockSpec(shape, lambda i: (0,) * len(shape))
    rows = lambda width, at=0: pl.BlockSpec((batch, CHUNK, width), lambda i: (0, i, at))
    return pl.pallas_call(
        functools.partial(scan_kernel, heads, inner, state),
        grid=(length // CHUNK,),
        in_specs=[
            rows(mix),
            rows(LANES, step_at),
            whole((batch, 8, mix)),
            whole((CONV, mix)),
            whole((1, LANES)),
            whole((1, LANES)),
            pl.BlockSpec(memory_space=pltpu.SMEM),
        ],
        out_specs=[
            rows(inner),
            rows(state),
            rows(LANES),
            whole((batch, inner, state)),
            whole((batch, 8, LANES)),
        ],
        out_shape=[
            jax.ShapeDtypeStruct((batch, length, inner), F32),
            jax.ShapeDtypeStruct((batch, length, state), BF16),
            jax.ShapeDtypeStruct((batch, length, LANES), F32),
            jax.ShapeDtypeStruct((batch, inner, state), F32),
            jax.ShapeDtypeStruct((batch, 8, LANES), F32),
        ],
        scratch_shapes=[
            pltpu.VMEM((batch, 8, mix), F32),
            pltpu.VMEM((batch, inner, state), F32),
            pltpu.VMEM((batch, 8, LANES), F32),
        ],
        cost_estimate=pl.CostEstimate(
            flops=2 * batch * length * inner * 4 * LANES, bytes_accessed=batch * length * 4096,
            transcendentals=batch * length * 2048,
        ),
        name="section_scan",
    )(proj, proj, before, taps, bias, rate, start)


def gate_kernel(heads, y_ref, c_ref, grow_ref, gate_ref, inc_ref, gain_ref, start_ref, g_ref, sq_ref):
    i = pl.program_id(0)
    batch, rows, inner = y_ref.shape
    line = lax.broadcasted_iota(jnp.int32, (rows, inner), 0) + i * rows
    for b in range(batch):
        carry = lax.dot_general(
            c_ref[b], inc_ref[b], (((1,), (1,)), ((), ())), preferred_element_type=F32
        )
        y = y_ref[b] + per_head(grow_ref[b], heads, inner // heads) * carry
        y = jnp.where(line >= start_ref[b], y, 0.0)
        gated = y * silu(gate_ref[b].astype(F32))
        sq_ref[b] = jnp.broadcast_to(jnp.sum(gated * gated, axis=1, keepdims=True), (rows, LANES))
        g_ref[b] = (gated * gain_ref[...]).astype(BF16)


def gate_section(y, cmat, grow, proj, incoming, gain, start, heads, mix):
    batch, length, inner = y.shape
    state = cmat.shape[2]
    rows = lambda width, at=0: pl.BlockSpec((batch, 2 * CHUNK, width), lambda i: (0, i, at))
    return pl.pallas_call(
        functools.partial(gate_kernel, heads),
        grid=(length // (2 * CHUNK),),
        in_specs=[
            rows(inner),
            rows(state),
            rows(LANES),
            rows(inner, mix // inner),
            pl.BlockSpec((batch, inner, state), lambda i: (0, 0, 0)),
            pl.BlockSpec((1, inner), lambda i: (0, 0)),
            pl.BlockSpec(memory_space=pltpu.SMEM),
        ],
        out_specs=[rows(inner), rows(LANES)],
        out_shape=[
            jax.ShapeDtypeStruct((batch, length, inner), BF16),
            jax.ShapeDtypeStruct((batch, length, LANES), F32),
        ],
        cost_estimate=pl.CostEstimate(
            flops=2 * batch * length * inner * LANES, bytes_accessed=batch * length * 3000,
            transcendentals=batch * length * inner,
        ),
        name="section_gate",
    )(y, cmat, grow, proj, incoming, gain, start)


def remote(src, dst, send_sem, recv_sem, axis, index):
    return pltpu.make_async_remote_copy(
        src_ref=src, dst_ref=dst, send_sem=send_sem, recv_sem=recv_sem,
        device_id={axis: index}, device_id_type=pl.DeviceIdType.MESH,
    )


def greet(axes):
    barrier = pltpu.get_barrier_semaphore()
    count = 0
    for axis in axes:
        n = lax.axis_size(axis)
        me = lax.axis_index(axis)
        for o in range(1, n):
            pl.semaphore_signal(
                barrier, inc=1, device_id={axis: lax.rem(me + o, n)},
                device_id_type=pl.DeviceIdType.MESH,
            )
        count += n - 1
    pl.semaphore_wait(barrier, count)


def line_gather(x_ref, got, sems, recv, use, pieces, between):
    left_sem, right_sem, side_sem = sems
    n = lax.axis_size("head")
    chips = n // 2
    me = lax.axis_index("head")
    chip, core = me // 2, me % 2
    other = chip * 2 + 1 - core
    rows = x_ref.shape[0] // pieces

    def at(j):
        return pl.ds(pl.multiple_of(j * rows, rows), rows)

    def passed_on(src, slot, j, sem, index):
        return remote(src, got.at[slot, at(j)], sem.at[slot, j], recv.at[slot, j], "head", index)

    def arrived(slot, j):
        passed_on(got.at[slot, at(j)], slot, j, side_sem, other).wait_recv()

    def on_right(src, slot, j):
        return passed_on(src, slot, j, right_sem, me + 2)

    def on_left(src, slot, j):
        return passed_on(src, slot, j, left_sem, me - 2)

    def on_side(src, slot, j):
        return passed_on(src, slot, j, side_sem, other)

    has_right, has_left = chip + 1 < chips, chip > 0

    @pl.loop(0, pieces)
    def _(j):
        @pl.when(has_right)
        def _():
            on_right(x_ref.at[at(j)], me, j).start()

        @pl.when(has_left)
        def _():
            on_left(x_ref.at[at(j)], me, j).start()

        on_side(x_ref.at[at(j)], me, j).start()

    between(0)

    @pl.loop(0, pieces)
    def _(j):
        use(x_ref[at(j), :], me, at(j))

    def from_side(d, j):
        def here(q):
            slot = q * 2 + 1 - core
            arrived(slot, j)
            use(got[slot, at(j), :], slot, at(j))

        @pl.when(chip - d >= 0)
        def _():
            here(chip - d)

        @pl.when((chip + d < chips) & (d > 0))
        def _():
            here(chip + d)

    def step(t):
        d, j = t // pieces + 1, t % pieces
        low, high = (chip - d) * 2 + core, (chip + d) * 2 + core

        @pl.when(chip - d >= 0)
        def _():
            arrived(low, j)
            block = got.at[low, at(j)]

            @pl.when(has_right)
            def _():
                on_right(block, low, j).start()

            on_side(block, low, j).start()

        @pl.when(chip + d < chips)
        def _():
            arrived(high, j)
            block = got.at[high, at(j)]

            @pl.when(has_left)
            def _():
                on_left(block, high, j).start()

            on_side(block, high, j).start()

        @pl.when(chip - d >= 0)
        def _():
            use(got[low, at(j), :], low, at(j))

        @pl.when(chip + d < chips)
        def _():
            use(got[high, at(j), :], high, at(j))

        from_side(d - 1, j)

    pl.loop(0, pieces)(step)
    between(1)
    pl.loop(pieces, (chips - 1) * pieces)(step)

    @pl.loop(0, pieces)
    def _(j):
        from_side(chips - 1, j)

    @pl.loop(0, chips * pieces)
    def _(t):
        q, j = t // pieces, t % pieces
        slot = q * 2 + core
        block = got.at[slot, at(j)]
        on_side(block, slot, j).wait_send()

        @pl.when(has_right & (q <= chip))
        def _():
            on_right(block, slot, j).wait_send()

        @pl.when(has_left & (q >= chip))
        def _():
            on_left(block, slot, j).wait_send()

    between(2)


def project_kernel(
    pieces, x_ref, w_ref, wo_ref, out_ref, cols_ref,
    got, total, left_sem, right_sem, side_sem, recv, out_send, out_recv, seq_send, seq_recv, own_sem,
):
    n, n_seq = lax.axis_size("head"), lax.axis_size("seq")
    me, sec = lax.axis_index("head"), lax.axis_index("seq")
    part, width = cols_ref.shape[2:]
    greet(("head", "seq"))

    def columns(to):
        return wo_ref.at[
            pl.ds(pl.multiple_of(sec * part, part), part), pl.ds(pl.multiple_of(to * width, width), width)
        ]

    def spread(o):
        to = lax.rem(me + o, n)
        return remote(columns(to), cols_ref.at[sec, me], out_send.at[o], out_recv.at[me], "head", to)

    def landed(o):
        frm = lax.rem(me + o, n)
        remote(
            columns(frm), cols_ref.at[sec, frm], out_send.at[o], out_recv.at[frm], "head", frm
        ).wait_recv()

    def shared(o):
        to = lax.rem(sec + o, n_seq)
        return remote(cols_ref.at[sec], cols_ref.at[sec], seq_send.at[o], seq_recv.at[sec], "seq", to)

    def got_share(o):
        frm = lax.rem(sec + o, n_seq)
        remote(
            cols_ref.at[frm], cols_ref.at[frm], seq_send.at[o], seq_recv.at[frm], "seq", frm
        ).wait_recv()

    def own_copy():
        return pltpu.make_async_copy(columns(me), cols_ref.at[sec, me], own_sem)

    def between(stage):
        if stage == 0:
            own_copy().start()
            pl.loop(1, n)(lambda o: spread(o).start())
        elif stage == 1:
            own_copy().wait()
            pl.loop(1, n)(landed)
            pl.loop(1, n_seq)(lambda o: shared(o).start())
        else:
            pl.loop(1, n)(lambda o: spread(o).wait_send())
            pl.loop(1, n_seq)(lambda o: shared(o).wait_send())
            pl.loop(1, n_seq)(got_share)

    total[...] = jnp.zeros_like(total)

    def use(block, slot, at):
        total[at, :] += jnp.dot(block, w_ref[slot], preferred_element_type=F32)

    line_gather(x_ref, got, (left_sem, right_sem, side_sem), recv, use, pieces, between)

    @pl.loop(0, pieces)
    def _(j):
        rows = x_ref.shape[0] // pieces
        at = pl.ds(pl.multiple_of(j * rows, rows), rows)
        out_ref[at, :] = total[at, :].astype(BF16)


def mix_kernel(
    pieces, x_ref, sq_ref, w_ref, out_ref, sums_ref,
    got, left_sem, right_sem, side_sem, recv, sq_send, sq_recv, own_sem,
):
    n = lax.axis_size("head")
    me = lax.axis_index("head")
    parts, _, part, width = w_ref.shape
    greet(("head",))

    def sums_to(o):
        to = lax.rem(me + o, n)
        return remote(sq_ref, sums_ref.at[me], sq_send.at[o], sq_recv.at[me], "head", to)

    def sums_from(o):
        frm = lax.rem(me + o, n)
        remote(sq_ref, sums_ref.at[frm], sq_send.at[o], sq_recv.at[frm], "head", frm).wait_recv()

    def own_copy():
        return pltpu.make_async_copy(sq_ref, sums_ref.at[me], own_sem)

    def between(stage):
        if stage == 0:
            own_copy().start()
            pl.loop(1, n)(lambda o: sums_to(o).start())
        elif stage == 2:
            own_copy().wait()
            pl.loop(1, n)(lambda o: sums_to(o).wait_send())
            pl.loop(1, n)(sums_from)

    out_ref[...] = jnp.zeros_like(out_ref)

    def use(block, slot, at):
        weights = w_ref[:, slot].reshape(parts * part, width)
        out_ref[at, :] += jnp.dot(block, weights, preferred_element_type=F32)

    line_gather(x_ref, got, (left_sem, right_sem, side_sem), recv, use, pieces, between)


VMEM_SPEC = pl.BlockSpec(memory_space=pltpu.VMEM)


def gather_scratch(n, rows, width, pieces):
    sem = pltpu.SemaphoreType.DMA((n, pieces))
    return [pltpu.VMEM((n, rows, width), BF16)], [sem, sem, sem, sem]


def gather_project(x, weights, w_out, pieces=8):
    rows, width = x.shape
    n, n_seq = lax.axis_size("head"), lax.axis_size("seq")
    wide = weights.shape[2]
    depth, model = w_out.shape
    slots, sems = gather_scratch(n, rows, width, pieces)
    dma = pltpu.SemaphoreType.DMA
    return pl.pallas_call(
        functools.partial(project_kernel, pieces),
        in_specs=[VMEM_SPEC] * 3,
        out_specs=[VMEM_SPEC] * 2,
        out_shape=[
            jax.ShapeDtypeStruct((rows, wide), BF16),
            jax.ShapeDtypeStruct((n_seq, n, depth // n_seq, model // n), BF16),
        ],
        scratch_shapes=slots
        + [pltpu.VMEM((rows, wide), F32)]
        + sems
        + [dma((n,)), dma((n,)), dma((n_seq,)), dma((n_seq,)), dma(())],
        compiler_params=pltpu.CompilerParams(
            collective_id=0, has_side_effects=True, vmem_limit_bytes=56 * 2**20
        ),
        name="gather_project",
    )(x, weights, w_out)


def gather_mix(g, squares, w_cols, pieces=8):
    rows, width = g.shape
    n = lax.axis_size("head")
    slots, sems = gather_scratch(n, rows, width, pieces)
    dma = pltpu.SemaphoreType.DMA
    return pl.pallas_call(
        functools.partial(mix_kernel, pieces),
        in_specs=[VMEM_SPEC] * 3,
        out_specs=[VMEM_SPEC] * 2,
        out_shape=[
            jax.ShapeDtypeStruct((rows, w_cols.shape[3]), F32),
            jax.ShapeDtypeStruct((n,) + squares.shape, F32),
        ],
        scratch_shapes=slots + sems + [dma((n,)), dma((n,)), dma(())],
        compiler_params=pltpu.CompilerParams(
            collective_id=1, has_side_effects=True, vmem_limit_bytes=48 * 2**20
        ),
        name="gather_mix",
    )(g, squares, w_cols)


def high_low(x):
    high = x.astype(BF16)
    return high, (x - high.astype(F32)).astype(BF16)


def per_device(
    tokens, w_gate, w_value, w_bc, w_step, step_bias, rate, conv_value, conv_bc, norm_gain,
    w_out, kept_states, kept_index, cached_len,
):
    batch, sec_len, d_part = tokens.shape
    inner = w_gate.shape[1]
    heads = w_step.shape[1]
    size = inner // heads
    state = w_bc.shape[1] // 2
    mix = inner + 2 * state
    slots = kept_states.shape[0]
    n_seq = lax.axis_size("seq")
    n_head = lax.axis_size("head")
    sec = lax.axis_index("seq")

    weights = jnp.concatenate(
        [w_value, w_bc, w_gate, jnp.pad(w_step, ((0, 0), (0, LANES - heads)))], axis=1
    ).reshape(n_head, d_part, -1)
    taps = jnp.concatenate([conv_value, conv_bc], axis=1)
    bias = jnp.pad(step_bias, (0, LANES - heads))[None]
    rates = jnp.pad(rate, (0, LANES - heads))[None]
    picked = jnp.stack(
        [lax.dynamic_index_in_dim(kept_states, kept_index[b] % slots, 0, False) for b in range(batch)]
    ).astype(BF16).reshape(batch, inner, state)
    start = cached_len - sec * sec_len

    proj, w_cols = gather_project(tokens.reshape(batch * sec_len, d_part), weights, w_out)
    proj = proj.reshape(batch, sec_len, -1)
    before = lax.ppermute(
        proj[:, sec_len - 8 :, :mix], "seq", [(i, i + 1) for i in range(n_seq - 1)]
    )
    y, cmat, grow, sec_state, total = scan_section(
        proj, before, taps, bias, rates, start, heads, inner, state
    )
    high, low = high_low(total)
    sent = jnp.concatenate([sec_state.astype(BF16), high, low, picked], axis=1)
    got = lax.all_gather(sent, "seq", axis=0)
    incoming = jnp.stack(
        [
            lax.dynamic_index_in_dim(got[:, b, inner + 16 :], kept_index[b] // slots, 0, False)
            for b in range(batch)
        ]
    )
    incoming = incoming.astype(F32).reshape(batch, heads, size, state)
    for r in range(n_seq - 1):
        decay = got[r, :, inner, :heads].astype(F32) + got[r, :, inner + 8, :heads].astype(F32)
        later = decay[:, :, None, None] * incoming + got[r, :, :inner].astype(F32).reshape(
            batch, heads, size, state
        )
        incoming = jnp.where(r < sec, later, incoming)
    g, squares = gate_section(
        y, cmat, grow, proj, incoming.reshape(batch, inner, state).astype(BF16),
        norm_gain[None], start, heads, mix,
    )
    mixed, sums = gather_mix(
        g.reshape(batch * sec_len, inner), squares[:, :, 0].reshape(-1, LANES), w_cols
    )
    meansq = jnp.sum(sums, axis=0).reshape(-1) / (inner * n_head)
    out = (mixed * lax.rsqrt(meansq + 1e-05)[:, None]).astype(BF16)
    return out.reshape(batch, sec_len, d_part)


def solution(mesh):
    return jax.shard_map(
        per_device,
        mesh=mesh,
        in_specs=(
            P(None, "seq", "head"),
            P(None, "head"),
            P(None, "head"),
            P(),
            P(None, "head"),
            P("head"),
            P("head"),
            P(None, "head"),
            P(),
            P("head"),
            P("head", None),
            P("seq", "head", None, None),
            P(),
            P(),
        ),
        out_specs=P(None, "seq", "head"),
        check_vma=False,
    )
```

time: 470 us -> 340 us (0.72)
  Pallas kernels: 27.3 us -> 267 us
  blocking collectives: 222 us -> 0 us
  waiting for transfers between devices: 131 us -> 25.1 us
  matrix products: 37 us -> 0 us
  local copies, waits for them, and re-layouts: 14.7 us -> 9.17 us
    pallas_call x2 -> x3, Pallas kernels: 8.75 us -> 251 us  [the longest x1 164 us: gather_project(): pl.pallas_call(functools.partial(project_kernel, pieces), in_specs=[VMEM_...]
    all_gather x5 -> x0, blocking collectives: 140 us -> none  [the longest x2 112 us: per_device(): sq_all = lax.all_gather(squares[:, 0], 'head', axis=0)]
    all_gather x4 -> x1, waiting for transfers between devices: 131 us -> 25.1 us  [per_device(): got = lax.all_gather(sent, 'seq', axis=0)]
    all_to_all x1 -> x0, blocking collectives: 82.2 us -> none  [per_device(): lax.all_to_all(w_out, 'head', split_axis=1, concat_axis=0, tiled=True)]
    dot_general x4 -> x0, matrix products: 37 us -> none  [the longest x2 28 us: per_device(): proj = jnp.dot(pieces[b], weights, preferred_element_type=F32).astype(BF16)]
    concatenate x2 -> x3, other arithmetic: 0.01 us -> 7.46 us  [the longest x1 6.14 us: per_device(): jnp.concatenate([w_value, w_bc, w_gate, jnp.pad(w_step, ((0, 0), (0, LANE...]
    all_gather x2 -> x0, other arithmetic: 6.67 us -> none  [per_device(): sq_all = lax.all_gather(squares[:, 0], 'head', axis=0)]
    pallas_call x2 -> x1, Pallas kernels: 18.5 us -> 15.6 us  [scan_section(): pl.pallas_call(functools.partial(scan_kernel, heads, inner, state), grid=...]
  transfers between devices with their start and end apart: 6 -> 2, of which waited for: 2 -> 1; matrix products, arithmetic and copies ran while one was open for 11% -> 1% of each run, Pallas kernels for 3% -> 0%
where the time goes in v2:
time: 340 us; the launch traced here: 337 us
  Pallas kernels  267 us (79%)
  waiting for transfers between devices  25.1 us (7%)
  between operations  18.4 us (5%)
  other arithmetic  16.3 us (5%)
  local copies, waits for them, and re-layouts  9.17 us (3%)
    pallas_call x1, Pallas kernels, gather_project(): pl.pallas_call(functools.partial(project_kernel, pieces), in_specs=[VMEM_...  164 us
    pallas_call x1, Pallas kernels, gather_mix(): pl.pallas_call(functools.partial(mix_kernel, pieces), in_specs=[VMEM_SPEC...  81.4 us
    all_gather x1, waiting for transfers between devices, per_device(): got = lax.all_gather(sent, 'seq', axis=0)  25.1 us
    pallas_call x1, Pallas kernels, scan_section(): pl.pallas_call(functools.partial(scan_kernel, heads, inner, state), grid=...  15.6 us
  transfers between devices with their start and end apart: 2, of which 1 were waited for; matrix products, arithmetic and copies ran while one was open for 1% of the time, Pallas kernels for 0%

profile of v2, /device:TPU:6, one launch (start us, length us, event | category | flops | bytes accessed | tf_op | source)
XLA Modules:
  0.0 337.3 jit_solution(3083553348428629896)
XLA Ops:
  6.5 1.3 copy.18
  7.8 6.1 %fusion.1 = bf16[4096,896]{1,0:T(8,128)(2,1)} fusion(bf16[4096,4]{1,0:T(8,128)(2,1)S(1)} %copy.18, bf16[4096,256]{1,0:T(8,128)(2,1)} %param.15, bf16[4096,256]{1,0:T(8,128)(2,1)} %param.17, bf16[4096,256]{1,0:T(8,128)(2,1)} %param.16), kind=kLoop, calls=%fused_computation.2 | loop fusion | flops 36700160 | bytes 13664256 | tf_op jit(solution)/shard_map/concatenate | solution.py:515
  14.0 164.1 %gather_project.1 = (bf16[2048,896]{1,0:T(8,128)(2,1)}, bf16[4,8,64,512]{3,2,1,0:T(8,128)(2,1)}) custom-call(bf16[2048,512]{1,0:T(8,128)(2,1)} %bitcast.45, bf16[8,512,896]{2,1,0:T(8,128)(2,1)} %bitcast.40, bf16[256,4096]{1,0:T(8,128)(2,1)} %wo_ref.1), custom_call_target="tpu_custom_call" | custom-call | tf_op jit(solution)/shard_map/gather_project/pallas_call | solution.py:455
  178.1 0.7 slice.62
  178.8 1.3 collective-permute-start
  180.1 0.6 fusion.10
  184.3 0.6 pad_maximum_fusion.taps_ref
  184.9 0.6 broadcast_subtract_fusion.start_ref
  185.5 1.0 dynamic-slice_convert_fusion.1
  186.5 0.6 pad_bitcast_fusion
  187.1 0.6 copy-done.7
  187.7 15.6 %section_scan.1 = (f32[2,1024,256]{2,1,0:T(8,128)}, bf16[2,1024,128]{2,1,0:T(8,128)(2,1)}, f32[2,1024,128]{2,1,0:T(8,128)}, f32[2,256,128]{2,1,0:T(8,128)}, f32[2,8,128]{2,1,0:T(8,128)}) custom-call(bf16[2,1024,896]{2,1,0:T(8,128)(2,1)} %bitcast.42, bf16[2,1024,896]{2,1,0:T(8,128)(2,1)} %bitcast.43, bf16[2,8,512]{2,1,0:T(8,128)(2,1)} %copy-done.7, ...), custom_call_target="tpu_custom_call" | custom-call | flops 536870912 | bytes 8388608 | tf_op jit(solution)/shard_map/section_scan/pallas_call | solution.py:110
  203.3 0.8 subtract_convert_fusion
  204.1 1.0 convert_element_type.102
  205.1 0.7 maximum_maximum_fusion
  207.1 25.1 %all-gather.3.cloned.1.call-done = bf16[8,528,128]{2,1,0:T(8,128)(2,1)} async-done(((bf16[2,528,128]{2,1,0:T(8,128)(2,1)}), bf16[8,528,128]{2,1,0:T(8,128)(2,1)}) %all-gather.3.cloned.1.call-update) | async-done | bytes 1081360 | tf_op jit(solution)/shard_map/all_gather | solution.py:536
  232.2 1.1 fusion.9
  233.3 0.7 fusion.8
  234.5 2.0 fusion.4.inc_ref
  236.4 5.9 %section_gate.1 = (bf16[2,1024,256]{2,1,0:T(8,128)(2,1)}, f32[2,1024,128]{2,1,0:T(8,128)}) custom-call(f32[2,1024,256]{2,1,0:T(8,128)} %get-tuple-element.17.y_ref, bf16[2,1024,128]{2,1,0:T(8,128)(2,1)} %get-tuple-element.18.c_ref, f32[2,1024,128]{2,1,0:T(8,128)} %get-tuple-element.19.grow_ref, bf16[2,1024,896]{2,1,0:T(8,128)(2,1)} %bitcast.44, ...), custom_call_target="tpu_custom_call" | custom-call | flops 134217728 | bytes 6144000 | tf_op jit(solution)/shard_map/section_gate/pallas_call | solution.py:168
  242.4 1.6 slice_reduce_fusion
  244.0 1.2 copy-done.1
  245.2 81.4 %gather_mix.1 = (f32[2048,512]{1,0:T(8,128)}, f32[8,16,128]{2,1,0:T(8,128)S(1)}) custom-call(bf16[2048,256]{1,0:T(8,128)(2,1)S(1)} %bitcast.39, f32[16,128]{1,0:T(8,128)S(1)} %reshape_squeeze.3.sq_ref, bf16[4,8,64,512]{3,2,1,0:T(8,128)(2,1)S(1)} %copy-done), custom_call_target="tpu_custom_call" | custom-call | tf_op jit(solution)/shard_map/gather_mix/pallas_call | solution.py:479
  326.6 3.8 %multiply_convert_fusion = bf16[2048,512]{1,0:T(8,128)(2,1)} fusion(f32[2048,512]{1,0:T(8,128)} %get-tuple-element.25, f32[2048]{0:T(1024)S(1)} %rsqrt_bitcast_fusion), kind=kLoop, calls=%fused_computation.3 | loop fusion | flops 2097152 | bytes 6299648 | tf_op jit(solution)/shard_map/convert_element_type | solution.py:558
  (30 shorter events, 0.6 us)
Async XLA Ops:
  6.5 225.6 %all-gather.3.cloned.1.call-start = ((), (), s32[]{:S(2)}) async-start(), calls=%async_computation | async-start | bytes 1351680 | tf_op jit(solution)/shard_map/all_gather | solution.py:536
  13.9 166.1 %copy-start.4 = (s32[2]{0:T(128)S(1)}, s32[2]{0:T(128)}, u32[]{:S(2)}) copy-start(s32[2]{0:T(128)} %param.26) | copy-start | bytes 28
  14.0 170.3 %copy-start.2 = (f32[4,256]{1,0:T(4,128)S(1)}, f32[4,256]{1,0:T(4,128)}, u32[]{:S(2)}) copy-start(f32[4,256]{1,0:T(4,128)} %param.22) | copy-start | bytes 12292
  14.0 170.4 %copy-start.3 = (f32[4,256]{1,0:T(4,128)S(1)}, f32[4,256]{1,0:T(4,128)}, u32[]{:S(2)}) copy-start(f32[4,256]{1,0:T(4,128)} %param.21) | copy-start | bytes 12292
  14.0 171.0 %copy-start.8 = (s32[2]{0:T(128)S(1)}, s32[2]{0:T(128)}, u32[]{:S(2)}) copy-start(s32[2]{0:T(128)} %param.27) | copy-start | bytes 28
  14.0 172.5 %copy-start.5 = (f32[4]{0:T(128)S(1)}, f32[4]{0:T(128)}, u32[]{:S(2)}) copy-start(f32[4]{0:T(128)} %param.20) | copy-start | bytes 52
  14.0 172.5 %copy-start.6 = (f32[4]{0:T(128)S(1)}, f32[4]{0:T(128)}, u32[]{:S(2)}) copy-start(f32[4]{0:T(128)} %param.19) | copy-start | bytes 52
  178.8 8.3 %collective-permute-start = (bf16[2,8,512]{2,1,0:T(8,128)(2,1)S(1)}, bf16[2,8,512]{2,1,0:T(8,128)(2,1)S(1)}, u32[]{:S(2)}, u32[]{:S(2)}) collective-permute-start(bf16[2,8,512]{2,1,0:T(8,128)(2,1)S(1)} %slice.62), channel_id=1, source_target_pairs={{0,8},{8,16},{16,24},{1,9},{9,17},{17,25},{2,10},{10,18},{18,26},{... | collective-permute-start | bytes 49160 | tf_op jit(solution)/shard_map/ppermute | solution.py:528
  187.1 0.6 copy-start.7
  236.4 7.5 %copy-start = (bf16[4,8,64,512]{3,2,1,0:T(8,128)(2,1)S(1)}, bf16[4,8,64,512]{3,2,1,0:T(8,128)(2,1)}, u32[]{:S(2)}) copy-start(bf16[4,8,64,512]{3,2,1,0:T(8,128)(2,1)} %get-tuple-element.24.w_ref) | copy-start | bytes 6291460
  244.0 1.2 copy-start.1
Sparse Core Ops, SparseCore 0:
  205.9 26.1 all-gather.2

commit v3 on v2

--- a/solution.py
+++ b/solution.py
@@ -39,7 +39,7 @@
 
     @pl.when(i == 0)
     def _():
-        tail[...] = before_ref[...].astype(F32)
+        tail[...] = before_ref[:, 8:, :].astype(F32)
         held[...] = jnp.zeros_like(held)
         passed[...] = jnp.zeros_like(passed)
 
@@ -104,7 +104,7 @@
 def scan_section(proj, before, taps, bias, rate, start, heads, inner, state):
     batch, length = proj.shape[:2]
     mix = inner + 2 * state
-    step_at = (mix + inner) // LANES
+    step_at = mix // LANES
     whole = lambda shape: pl.BlockSpec(shape, lambda i: (0,) * len(shape))
     rows = lambda width, at=0: pl.BlockSpec((batch, CHUNK, width), lambda i: (0, i, at))
     return pl.pallas_call(
@@ -113,7 +113,7 @@
         in_specs=[
             rows(mix),
             rows(LANES, step_at),
-            whole((batch, 8, mix)),
+            whole((batch, 16, mix)),
             whole((CONV, mix)),
             whole((1, LANES)),
             whole((1, LANES)),
@@ -146,50 +146,6 @@
     )(proj, proj, before, taps, bias, rate, start)
 
 
-def gate_kernel(heads, y_ref, c_ref, grow_ref, gate_ref, inc_ref, gain_ref, start_ref, g_ref, sq_ref):
-    i = pl.program_id(0)
-    batch, rows, inner = y_ref.shape
-    line = lax.broadcasted_iota(jnp.int32, (rows, inner), 0) + i * rows
-    for b in range(batch):
-        carry = lax.dot_general(
-            c_ref[b], inc_ref[b], (((1,), (1,)), ((), ())), preferred_element_type=F32
-        )
-        y = y_ref[b] + per_head(grow_ref[b], heads, inner // heads) * carry
-        y = jnp.where(line >= start_ref[b], y, 0.0)
-        gated = y * silu(gate_ref[b].astype(F32))
-        sq_ref[b] = jnp.broadcast_to(jnp.sum(gated * gated, axis=1, keepdims=True), (rows, LANES))
-        g_ref[b] = (gated * gain_ref[...]).astype(BF16)
-
-
-def gate_section(y, cmat, grow, proj, incoming, gain, start, heads, mix):
-    batch, length, inner = y.shape
-    state = cmat.shape[2]
-    rows = lambda width, at=0: pl.BlockSpec((batch, 2 * CHUNK, width), lambda i: (0, i, at))
-    return pl.pallas_call(
-        functools.partial(gate_kernel, heads),
-        grid=(length // (2 * CHUNK),),
-        in_specs=[
-            rows(inner),
-            rows(state),
-            rows(LANES),
-            rows(inner, mix // inner),
-            pl.BlockSpec((batch, inner, state), lambda i: (0, 0, 0)),
-            pl.BlockSpec((1, inner), lambda i: (0, 0)),
-            pl.BlockSpec(memory_space=pltpu.SMEM),
-        ],
-        out_specs=[rows(inner), rows(LANES)],
-        out_shape=[
-            jax.ShapeDtypeStruct((batch, length, inner), BF16),
-            jax.ShapeDtypeStruct((batch, length, LANES), F32),
-        ],
-        cost_estimate=pl.CostEstimate(
-            flops=2 * batch * length * inner * LANES, bytes_accessed=batch * length * 3000,
-            transcendentals=batch * length * inner,
-        ),
-        name="section_gate",
-    )(y, cmat, grow, proj, incoming, gain, start)
-
-
 def remote(src, dst, send_sem, recv_sem, axis, index):
     return pltpu.make_async_remote_copy(
         src_ref=src, dst_ref=dst, send_sem=send_sem, recv_sem=recv_sem,
@@ -212,7 +168,7 @@
     pl.semaphore_wait(barrier, count)
 
 
-def line_gather(x_ref, got, sems, recv, use, pieces, between):
+def line_gather(x_ref, got, sems, recv, use, pieces, between, prepare=None):
     left_sem, right_sem, side_sem = sems
     n = lax.axis_size("head")
     chips = n // 2
@@ -243,6 +199,9 @@
 
     @pl.loop(0, pieces)
     def _(j):
+        if prepare is not None:
+            prepare(j, at(j))
+
         @pl.when(has_right)
         def _():
             on_right(x_ref.at[at(j)], me, j).start()
@@ -336,13 +295,28 @@
 
 
 def project_kernel(
-    pieces, x_ref, w_ref, wo_ref, out_ref, cols_ref,
-    got, total, left_sem, right_sem, side_sem, recv, out_send, out_recv, seq_send, seq_recv, own_sem,
+    pieces, batch, inner, x_ref, value_ref, bc_ref, step_ref, gate_w_ref, wo_ref, kept_ref,
+    mixin_ref, gate_ref, cols_ref, before_ref, pool_ref,
+    got, total, w, left_sem, right_sem, side_sem, recv, w_sem,
+    out_send, out_recv, seq_send, seq_recv, kept_send, kept_recv, tail_send, tail_recv, own_sem,
 ):
     n, n_seq = lax.axis_size("head"), lax.axis_size("seq")
     me, sec = lax.axis_index("head"), lax.axis_index("seq")
     part, width = cols_ref.shape[2:]
+    length = x_ref.shape[0] // batch
+    mix = value_ref.shape[2] + bc_ref.shape[2]
+    gate_at = mixin_ref.shape[1]
     greet(("head", "seq"))
+
+    def weight_copies():
+        copies, column = [], 0
+        for i, ref in enumerate((value_ref, bc_ref, step_ref, gate_w_ref)):
+            wide = ref.shape[2]
+            copies.append(
+                pltpu.make_async_copy(ref, w.at[:, :, column : column + wide], w_sem.at[i])
+            )
+            column += wide
+        return copies
 
     def columns(to):
         return wo_ref.at[
@@ -369,55 +343,155 @@
             cols_ref.at[frm], cols_ref.at[frm], seq_send.at[o], seq_recv.at[frm], "seq", frm
         ).wait_recv()
 
-    def own_copy():
-        return pltpu.make_async_copy(columns(me), cols_ref.at[sec, me], own_sem)
+    def kept_to(o):
+        to = lax.rem(sec + o, n_seq)
+        return remote(kept_ref, pool_ref.at[sec], kept_send.at[o], kept_recv.at[sec], "seq", to)
+
+    def kept_from(o):
+        frm = lax.rem(sec + o, n_seq)
+        remote(kept_ref, pool_ref.at[frm], kept_send.at[o], kept_recv.at[frm], "seq", frm).wait_recv()
+
+    def own_cols():
+        return pltpu.make_async_copy(columns(me), cols_ref.at[sec, me], own_sem.at[0])
+
+    def own_kept():
+        return pltpu.make_async_copy(kept_ref, pool_ref.at[sec], own_sem.at[1])
+
+    def tail_copy(b, index):
+        return remote(
+            mixin_ref.at[pl.ds((b + 1) * length - 16, 16), pl.ds(0, mix)],
+            before_ref.at[b], tail_send.at[b], tail_recv.at[b], "seq", index,
+        )
 
     def between(stage):
         if stage == 0:
-            own_copy().start()
+            copies = weight_copies()
+            for copy in copies:
+                copy.start()
+            own_cols().start()
+            own_kept().start()
             pl.loop(1, n)(lambda o: spread(o).start())
+            pl.loop(1, n_seq)(lambda o: kept_to(o).start())
+            total[...] = jnp.zeros_like(total)
+            for copy in copies:
+                copy.wait()
         elif stage == 1:
-            own_copy().wait()
+            own_cols().wait()
             pl.loop(1, n)(landed)
             pl.loop(1, n_seq)(lambda o: shared(o).start())
         else:
+            own_kept().wait()
             pl.loop(1, n)(lambda o: spread(o).wait_send())
             pl.loop(1, n_seq)(lambda o: shared(o).wait_send())
             pl.loop(1, n_seq)(got_share)
-
-    total[...] = jnp.zeros_like(total)
+            pl.loop(1, n_seq)(lambda o: kept_to(o).wait_send())
+            pl.loop(1, n_seq)(kept_from)
 
     def use(block, slot, at):
-        total[at, :] += jnp.dot(block, w_ref[slot], preferred_element_type=F32)
+        total[at, :] += jnp.dot(block, w[slot], preferred_element_type=F32)
 
     line_gather(x_ref, got, (left_sem, right_sem, side_sem), recv, use, pieces, between)
 
-    @pl.loop(0, pieces)
-    def _(j):
-        rows = x_ref.shape[0] // pieces
-        at = pl.ds(pl.multiple_of(j * rows, rows), rows)
-        out_ref[at, :] = total[at, :].astype(BF16)
+    for b in range(batch):
+        at = pl.ds((b + 1) * length - 16, 16)
+        mixin_ref[at, :] = total[at, :gate_at].astype(BF16)
+
+        @pl.when(sec + 1 < n_seq)
+        def _():
+            tail_copy(b, sec + 1).start()
+
+        @pl.when(sec == 0)
+        def _():
+            before_ref[b] = jnp.zeros(before_ref.shape[1:], BF16)
+
+    rows = length // (pieces // batch)
+    for b in range(batch):
+        for j in range(pieces // batch):
+            begin = b * length + j * rows
+            gate_ref[begin : begin + rows, :] = total[begin : begin + rows, gate_at:].astype(BF16)
+            end = min(begin + rows, (b + 1) * length - 16)
+            mixin_ref[begin:end, :] = total[begin:end, :gate_at].astype(BF16)
+
+    for b in range(batch):
+
+        @pl.when(sec + 1 < n_seq)
+        def _():
+            tail_copy(b, sec + 1).wait_send()
+
+        @pl.when(sec > 0)
+        def _():
+            tail_copy(b, sec - 1).wait_recv()
 
 
 def mix_kernel(
-    pieces, x_ref, sq_ref, w_ref, out_ref, sums_ref,
-    got, left_sem, right_sem, side_sem, recv, sq_send, sq_recv, own_sem,
+    pieces, heads, y_ref, c_ref, grow_ref, gate_ref, sent_ref, pool_ref, gain_ref, w_ref,
+    owner_ref, start_ref, out_ref, sums_ref,
+    got, x, sq, states, incoming, left_sem, right_sem, side_sem, recv,
+    sq_send, sq_recv, own_sem, st_send, st_recv,
 ):
-    n = lax.axis_size("head")
-    me = lax.axis_index("head")
+    n, n_seq = lax.axis_size("head"), lax.axis_size("seq")
+    me, sec = lax.axis_index("head"), lax.axis_index("seq")
     parts, _, part, width = w_ref.shape
-    greet(("head",))
+    batch, inner, state = pool_ref.shape[1:]
+    size = inner // heads
+    rows = x.shape[0] // pieces
+    length = x.shape[0] // batch
+    greet(("head", "seq"))
+
+    def state_copy(to, frm):
+        return remote(sent_ref, states.at[frm], st_send.at[to], st_recv.at[frm], "seq", to)
+
+    for r in range(n_seq):
+
+        @pl.when(sec < r)
+        def _():
+            state_copy(r, sec).start()
+
+    out_ref[...] = jnp.zeros_like(out_ref)
+    for b in range(batch):
+        first = owner_ref[0, b] * pool_ref[0, b].astype(F32)
+        for r in range(1, n_seq):
+            first = first + owner_ref[r, b] * pool_ref[r, b].astype(F32)
+        incoming[b] = first
+
+    for r in range(n_seq - 1):
+
+        @pl.when(sec > r)
+        def _():
+            state_copy(sec, r).wait_recv()
+            for b in range(batch):
+                decay = states[r, b, inner : inner + 16, :].astype(F32)
+                for h in range(heads):
+                    at = slice(h * size, (h + 1) * size)
+                    one = decay[0:1, h : h + 1] + decay[8:9, h : h + 1]
+                    incoming[b, at, :] = one * incoming[b, at, :] + states[r, b, at, :].astype(F32)
+
+    def prepare(j, at):
+        b = j // (pieces // batch)
+        carry = lax.dot_general(
+            c_ref[at, :], incoming[b].astype(BF16), (((1,), (1,)), ((), ())),
+            preferred_element_type=F32,
+        )
+        y = y_ref[at, :] + per_head(grow_ref[at, :], heads, size) * carry
+        line = lax.broadcasted_iota(jnp.int32, (rows, inner), 0) + (j * rows - b * length)
+        y = jnp.where(line >= start_ref[b], y, 0.0)
+        gated = y * silu(gate_ref[at, :].astype(F32))
+        x[at, :] = (gated * gain_ref[...]).astype(BF16)
+        sq[pl.ds(j, 1), :] = lax.dot_general(
+            jnp.ones((8, inner), F32), gated * gated, (((1,), (1,)), ((), ())),
+            precision=lax.Precision.HIGHEST, preferred_element_type=F32,
+        )[0:1, :]
 
     def sums_to(o):
         to = lax.rem(me + o, n)
-        return remote(sq_ref, sums_ref.at[me], sq_send.at[o], sq_recv.at[me], "head", to)
+        return remote(sq, sums_ref.at[me], sq_send.at[o], sq_recv.at[me], "head", to)
 
     def sums_from(o):
         frm = lax.rem(me + o, n)
-        remote(sq_ref, sums_ref.at[frm], sq_send.at[o], sq_recv.at[frm], "head", frm).wait_recv()
+        remote(sq, sums_ref.at[frm], sq_send.at[o], sq_recv.at[frm], "head", frm).wait_recv()
 
     def own_copy():
-        return pltpu.make_async_copy(sq_ref, sums_ref.at[me], own_sem)
+        return pltpu.make_async_copy(sq, sums_ref.at[me], own_sem)
 
     def between(stage):
         if stage == 0:
@@ -428,16 +502,22 @@
             pl.loop(1, n)(lambda o: sums_to(o).wait_send())
             pl.loop(1, n)(sums_from)
 
-    out_ref[...] = jnp.zeros_like(out_ref)
-
     def use(block, slot, at):
         weights = w_ref[:, slot].reshape(parts * part, width)
         out_ref[at, :] += jnp.dot(block, weights, preferred_element_type=F32)
 
-    line_gather(x_ref, got, (left_sem, right_sem, side_sem), recv, use, pieces, between)
+    line_gather(x, got, (left_sem, right_sem, side_sem), recv, use, pieces, between, prepare)
+
+    for r in range(n_seq):
+
+        @pl.when(sec < r)
+        def _():
+            state_copy(r, sec).wait_send()
 
 
 VMEM_SPEC = pl.BlockSpec(memory_space=pltpu.VMEM)
+SMEM_SPEC = pl.BlockSpec(memory_space=pltpu.SMEM)
+ANY_SPEC = pl.BlockSpec(memory_space=pl.ANY)
 
 
 def gather_scratch(n, rows, width, pieces):
@@ -445,51 +525,69 @@
     return [pltpu.VMEM((n, rows, width), BF16)], [sem, sem, sem, sem]
 
 
-def gather_project(x, weights, w_out, pieces=8):
+def gather_project(x, w_value, w_bc, w_step, w_gate, w_out, kept, pieces=8):
     rows, width = x.shape
     n, n_seq = lax.axis_size("head"), lax.axis_size("seq")
-    wide = weights.shape[2]
+    parts = [w.reshape(n, width, w.shape[1]) for w in (w_value, w_bc, w_step, w_gate)]
+    wide = sum(w.shape[2] for w in parts)
+    inner = w_gate.shape[1]
+    mix = w_value.shape[1] + w_bc.shape[1]
+    batch = kept.shape[0]
     depth, model = w_out.shape
     slots, sems = gather_scratch(n, rows, width, pieces)
     dma = pltpu.SemaphoreType.DMA
     return pl.pallas_call(
-        functools.partial(project_kernel, pieces),
-        in_specs=[VMEM_SPEC] * 3,
-        out_specs=[VMEM_SPEC] * 2,
+        functools.partial(project_kernel, pieces, batch, inner),
+        in_specs=[VMEM_SPEC] + [ANY_SPEC] * 4 + [VMEM_SPEC] * 2,
+        out_specs=[VMEM_SPEC] * 5,
         out_shape=[
-            jax.ShapeDtypeStruct((rows, wide), BF16),
+            jax.ShapeDtypeStruct((rows, wide - inner), BF16),
+            jax.ShapeDtypeStruct((rows, inner), BF16),
             jax.ShapeDtypeStruct((n_seq, n, depth // n_seq, model // n), BF16),
+            jax.ShapeDtypeStruct((batch, 16, mix), BF16),
+            jax.ShapeDtypeStruct((n_seq,) + kept.shape, BF16),
         ],
         scratch_shapes=slots
-        + [pltpu.VMEM((rows, wide), F32)]
+        + [pltpu.VMEM((rows, wide), F32), pltpu.VMEM((n, width, wide), BF16)]
         + sems
-        + [dma((n,)), dma((n,)), dma((n_seq,)), dma((n_seq,)), dma(())],
+        + [dma((4,)), dma((n,)), dma((n,))]
+        + [dma((n_seq,))] * 4
+        + [dma((batch,)), dma((batch,)), dma((2,))],
         compiler_params=pltpu.CompilerParams(
             collective_id=0, has_side_effects=True, vmem_limit_bytes=56 * 2**20
         ),
         name="gather_project",
-    )(x, weights, w_out)
-
-
-def gather_mix(g, squares, w_cols, pieces=8):
-    rows, width = g.shape
-    n = lax.axis_size("head")
-    slots, sems = gather_scratch(n, rows, width, pieces)
+    )(x, *parts, w_out, kept)
+
+
+def gather_mix(y, cmat, grow, gate, sent, pool, gain, w_cols, owner, start, heads, pieces=8):
+    rows, inner = y.shape
+    n, n_seq = lax.axis_size("head"), lax.axis_size("seq")
+    batch, state = pool.shape[1], pool.shape[3]
+    slots, sems = gather_scratch(n, rows, inner, pieces)
     dma = pltpu.SemaphoreType.DMA
     return pl.pallas_call(
-        functools.partial(mix_kernel, pieces),
-        in_specs=[VMEM_SPEC] * 3,
+        functools.partial(mix_kernel, pieces, heads),
+        in_specs=[VMEM_SPEC] * 8 + [SMEM_SPEC] * 2,
         out_specs=[VMEM_SPEC] * 2,
         out_shape=[
             jax.ShapeDtypeStruct((rows, w_cols.shape[3]), F32),
-            jax.ShapeDtypeStruct((n,) + squares.shape, F32),
+            jax.ShapeDtypeStruct((n, pieces, rows // pieces), F32),
         ],
-        scratch_shapes=slots + sems + [dma((n,)), dma((n,)), dma(())],
+        scratch_shapes=slots
+        + [
+            pltpu.VMEM((rows, inner), BF16),
+            pltpu.VMEM((pieces, rows // pieces), F32),
+            pltpu.VMEM((n_seq,) + sent.shape, BF16),
+            pltpu.VMEM((batch, inner, state), F32),
+        ]
+        + sems
+        + [dma((n,)), dma((n,)), dma(()), dma((n_seq,)), dma((n_seq,))],
         compiler_params=pltpu.CompilerParams(
             collective_id=1, has_side_effects=True, vmem_limit_bytes=48 * 2**20
         ),
         name="gather_mix",
-    )(g, squares, w_cols)
+    )(y, cmat, grow, gate, sent, pool, gain, w_cols, owner, start)
 
 
 def high_low(x):
@@ -512,9 +610,7 @@
     n_head = lax.axis_size("head")
     sec = lax.axis_index("seq")
 
-    weights = jnp.concatenate(
-        [w_value, w_bc, w_gate, jnp.pad(w_step, ((0, 0), (0, LANES - heads)))], axis=1
-    ).reshape(n_head, d_part, -1)
+    tokens_all = batch * sec_len
     taps = jnp.concatenate([conv_value, conv_bc], axis=1)
     bias = jnp.pad(step_bias, (0, LANES - heads))[None]
     rates = jnp.pad(rate, (0, LANES - heads))[None]
@@ -522,37 +618,21 @@
         [lax.dynamic_index_in_dim(kept_states, kept_index[b] % slots, 0, False) for b in range(batch)]
     ).astype(BF16).reshape(batch, inner, state)
     start = cached_len - sec * sec_len
-
-    proj, w_cols = gather_project(tokens.reshape(batch * sec_len, d_part), weights, w_out)
-    proj = proj.reshape(batch, sec_len, -1)
-    before = lax.ppermute(
-        proj[:, sec_len - 8 :, :mix], "seq", [(i, i + 1) for i in range(n_seq - 1)]
+    owner = (jnp.arange(n_seq)[:, None] == (kept_index // slots)[None, :]).astype(F32)
+
+    mixin, gate, w_cols, before, pool = gather_project(
+        tokens.reshape(tokens_all, d_part), w_value, w_bc,
+        jnp.pad(w_step, ((0, 0), (0, LANES - heads))), w_gate, w_out, picked,
     )
     y, cmat, grow, sec_state, total = scan_section(
-        proj, before, taps, bias, rates, start, heads, inner, state
+        mixin.reshape(batch, sec_len, -1), before, taps, bias, rates, start, heads, inner, state
     )
     high, low = high_low(total)
-    sent = jnp.concatenate([sec_state.astype(BF16), high, low, picked], axis=1)
-    got = lax.all_gather(sent, "seq", axis=0)
-    incoming = jnp.stack(
-        [
-            lax.dynamic_index_in_dim(got[:, b, inner + 16 :], kept_index[b] // slots, 0, False)
-            for b in range(batch)
-        ]
-    )
-    incoming = incoming.astype(F32).reshape(batch, heads, size, state)
-    for r in range(n_seq - 1):
-        decay = got[r, :, inner, :heads].astype(F32) + got[r, :, inner + 8, :heads].astype(F32)
-        later = decay[:, :, None, None] * incoming + got[r, :, :inner].astype(F32).reshape(
-            batch, heads, size, state
-        )
-        incoming = jnp.where(r < sec, later, incoming)
-    g, squares = gate_section(
-        y, cmat, grow, proj, incoming.reshape(batch, inner, state).astype(BF16),
-        norm_gain[None], start, heads, mix,
-    )
+    sent = jnp.concatenate([sec_state.astype(BF16), high, low], axis=1)
     mixed, sums = gather_mix(
-        g.reshape(batch * sec_len, inner), squares[:, :, 0].reshape(-1, LANES), w_cols
+        y.reshape(tokens_all, inner), cmat.reshape(tokens_all, state),
+        grow.reshape(tokens_all, LANES), gate, sent, pool, norm_gain[None], w_cols, owner, start,
+        heads,
     )
     meansq = jnp.sum(sums, axis=0).reshape(-1) / (inner * n_head)
     out = (mixed * lax.rsqrt(meansq + 1e-05)[:, None]).astype(BF16)

time: 340 us -> 292 us (0.86)
  waiting for transfers between devices: 25.1 us -> 0 us
  between operations: 18.4 us -> 3.99 us
  other arithmetic: 16.3 us -> 9.39 us
    all_gather x1 -> x0, waiting for transfers between devices: 25.1 us -> none  [per_device(): got = lax.all_gather(sent, 'seq', axis=0)]
    concatenate x2 -> x1, other arithmetic: 6.86 us -> 0.01 us  [per_device(): sent = jnp.concatenate([sec_state.astype(BF16), high, low], axis=1)]
    pallas_call x3 -> x2, Pallas kernels: 251 us -> 253 us  [the longest x1 164 us: gather_project(): pl.pallas_call(functools.partial(project_kernel, pieces, batch, inner), i...]
  transfers between devices with their start and end apart: 2 -> 0, of which waited for: 1 -> 0; matrix products, arithmetic and copies ran while one was open for 1% -> 0% of each run, Pallas kernels for 0% -> 0%
where the time goes in v3:
time: 292 us
  Pallas kernels  268 us (92%)
  local copies, waits for them, and re-layouts  9.89 us (3%)
  other arithmetic  9.39 us (3%)
  between operations  3.99 us (1%)
    pallas_call x1, Pallas kernels, gather_project(): pl.pallas_call(functools.partial(project_kernel, pieces, batch, inner), i...  164 us
    pallas_call x1, Pallas kernels, gather_mix(): pl.pallas_call(functools.partial(mix_kernel, pieces, heads), in_specs=[VM...  88.9 us
    pallas_call x1, Pallas kernels, scan_section(): pl.pallas_call(functools.partial(scan_kernel, heads, inner, state), grid=...  15.8 us

profile of v3, /device:TPU:6, one launch (start us, length us, event | category | flops | bytes accessed | tf_op | source)
XLA Modules:
  0.0 291.7 jit_solution(6948525937846923344)
XLA Ops:
  0.0 1.1 broadcast_subtract_fusion.start_ref
  1.1 0.7 and_select_fusion
  1.8 1.2 pad_bitcast_fusion
  3.0 1.4 fusion.1
  8.2 1.3 pad_maximum_fusion.2.taps_ref
  9.5 1.0 dynamic-slice_convert_fusion.1
  10.5 0.7 pad_maximum_fusion.1.kept_ref
  11.2 1.3 copy.16
  12.5 1.2 pad.11.clone
  13.6 163.8 %gather_project.1 = (bf16[2048,640]{1,0:T(8,128)(2,1)}, bf16[2048,256]{1,0:T(8,128)(2,1)}, bf16[4,8,64,512]{3,2,1,0:T(8,128)(2,1)}, bf16[2,16,512]{2,1,0:T(8,128)(2,1)}, bf16[4,2,256,128]{3,2,1,0:T(8,128)(2,1)}) custom-call(bf16[2048,512]{1,0:T(8,128)(2,1)} %bitcast.27, bf16[8,512,256]{2,1,0:T(8,128)(2,1)} %bitcast.28, bf16[8,512,256]{2,1,0:T(8,128)(2,1)} %bitcast.29, ...), custom_call_target="tpu_custom_call" | custom-call | tf_op jit(solution)/shard_map/gather_project/pallas_call | solution.py:539
  177.4 0.0 copy-start.1
  177.4 0.0 copy-start.3
  177.4 0.0 copy-start.5
  177.4 0.0 copy-start.6
  177.5 15.8 %section_scan.1 = (f32[2,1024,256]{2,1,0:T(8,128)}, bf16[2,1024,128]{2,1,0:T(8,128)(2,1)}, f32[2,1024,128]{2,1,0:T(8,128)}, f32[2,256,128]{2,1,0:T(8,128)}, f32[2,8,128]{2,1,0:T(8,128)}) custom-call(bf16[2,1024,640]{2,1,0:T(8,128)(2,1)} %bitcast.34, bf16[2,1024,640]{2,1,0:T(8,128)(2,1)} %bitcast.35, bf16[2,16,512]{2,1,0:T(8,128)(2,1)} %get-tuple-element.18.before_ref, ...), custom_call_target="tpu_custom_call" | custom-call | flops 536870912 | bytes 8388608 | tf_op jit(solution)/shard_map/section_scan/pallas_call | solution.py:110
  193.2 0.8 subtract_convert_fusion
  194.0 1.0 convert_element_type.25
  195.0 0.0 copy-done.1
  195.0 0.0 copy-start
  195.1 1.6 copy-done
  196.6 1.2 copy-done.2
  197.9 1.0 copy-done.4
  198.9 88.9 %gather_mix.1 = (f32[2048,512]{1,0:T(8,128)}, f32[8,8,256]{2,1,0:T(8,128)S(1)}) custom-call(f32[2048,256]{1,0:T(8,128)S(1)} %bitcast.22, bf16[2048,128]{1,0:T(8,128)(2,1)S(1)} %bitcast.24, f32[2048,128]{1,0:T(8,128)S(1)} %bitcast.23, bf16[2048,256]{1,0:T(8,128)(2,1)S(1)} %copy-done.1, bf16[2,272,128]{2,1,0:T(8,128)(2,1)S(1)} %pad_maximum_fusion.sent_ref, ...), custom_call_target="tpu_custom_call" | custom-call | tf_op jit(solution)/shard_map/gather_mix/pallas_call | solution.py:569
  287.9 3.8 %multiply_convert_fusion = bf16[2048,512]{1,0:T(8,128)(2,1)} fusion(f32[2048,512]{1,0:T(8,128)} %get-tuple-element.27, f32[2048]{0:T(1024)S(1)} %bitcast.33), kind=kLoop, calls=%fused_computation | loop fusion | flops 2097152 | bytes 6299648 | tf_op jit(solution)/shard_map/convert_element_type | solution.py:638
  (10 shorter events, 0.1 us)
Async XLA Ops:
  177.4 17.6 %copy-start.1 = (bf16[2048,256]{1,0:T(8,128)(2,1)S(1)}, bf16[2048,256]{1,0:T(8,128)(2,1)}, u32[]{:S(2)}) copy-start(bf16[2048,256]{1,0:T(8,128)(2,1)} %get-tuple-element.22.gate_ref) | copy-start | bytes 3145732
  177.4 17.6 %copy-start.3 = (bf16[4,2,256,128]{3,2,1,0:T(8,128)(2,1)S(1)}, bf16[4,2,256,128]{3,2,1,0:T(8,128)(2,1)}, u32[]{:S(2)}) copy-start(bf16[4,2,256,128]{3,2,1,0:T(8,128)(2,1)} %get-tuple-element.25.pool_ref) | copy-start | bytes 1572868
  177.4 17.6 %copy-start.5 = (f32[256]{0:T(256)S(1)}, f32[256]{0:T(256)}, u32[]{:S(2)}) copy-start(f32[256]{0:T(256)} %param.23) | copy-start | bytes 3076
  177.4 17.6 %copy-start.6 = (s32[2]{0:T(128)S(1)}, s32[2]{0:T(128)}, u32[]{:S(2)}) copy-start(s32[2]{0:T(128)} %broadcast_subtract_fusion.start_ref) | copy-start | bytes 28
  195.0 1.6 copy-start
  196.6 1.2 copy-start.2
  197.9 1.0 copy-start.4

commit v4 on v3

--- a/solution.py
+++ b/solution.py
@@ -15,7 +15,7 @@
 
 
 def silu(x):
-    return x * (1.0 / (1.0 + jnp.exp(-x)))
+    return x * (0.5 + 0.5 * jnp.tanh(0.5 * x))
 
 
 def softplus(x):
@@ -30,8 +30,8 @@
 
 
 def scan_kernel(
-    heads, inner, state, mixin_ref, step_ref, before_ref, taps_ref, bias_ref, rate_ref, start_ref,
-    y_ref, c_ref, grow_ref, sec_ref, total_ref, tail, held, passed,
+    heads, inner, state, mixin_ref, step_ref, before_ref, value_taps_ref, bc_taps_ref, bias_ref, rate_ref,
+    cached_ref, y_ref, c_ref, grow_ref, sent_ref, tail, held, passed,
 ):
     i = pl.program_id(0)
     batch, rows = mixin_ref.shape[:2]
@@ -46,24 +46,32 @@
     tri_r = lax.broadcasted_iota(jnp.int32, (rows, rows), 0)
     tri_c = lax.broadcasted_iota(jnp.int32, (rows, rows), 1)
     lower = tri_r >= tri_c
-    line = lax.broadcasted_iota(jnp.int32, (rows, LANES), 0) + i * rows
+    at_row = lax.axis_index("seq") * pl.num_programs(0) + i
+    line = lax.broadcasted_iota(jnp.int32, (rows, LANES), 0) + at_row * rows
+    lane = lax.broadcasted_iota(jnp.int32, (1, LANES), 1)
+    bias = jnp.zeros((1, LANES), F32)
+    rate = jnp.zeros((1, LANES), F32)
+    for h in range(heads):
+        bias = jnp.where(lane == h, bias_ref[h], bias)
+        rate = jnp.where(lane == h, rate_ref[h], rate)
+    taps = jnp.concatenate([value_taps_ref[...], bc_taps_ref[...]], axis=1)
     for b in range(batch):
         mixin = mixin_ref[b].astype(F32)
         padded = jnp.concatenate([tail[b], mixin], axis=0)
         tail[b] = mixin[rows - 8 :, :]
         first = 8 - CONV + 1
-        conv = taps_ref[0:1, :] * padded[first : first + rows, :]
+        conv = taps[0:1, :] * padded[first : first + rows, :]
         for k in range(1, CONV):
-            conv = conv + taps_ref[k : k + 1, :] * padded[first + k : first + k + rows, :]
+            conv = conv + taps[k : k + 1, :] * padded[first + k : first + k + rows, :]
         conv = silu(conv)
         xs = conv[:, :inner]
         bmat = conv[:, inner : inner + state].astype(BF16)
         cmat = conv[:, inner + state :].astype(BF16)
         c_ref[b] = cmat
-        dt = softplus(step_ref[b].astype(F32) + bias_ref[...])
-        dt = jnp.where(line >= start_ref[b], dt, 0.0)
+        dt = softplus(step_ref[b].astype(F32) + bias)
+        dt = jnp.where(line >= cached_ref[b], dt, 0.0)
         cumul = jnp.dot(
-            lower.astype(F32), -dt * rate_ref[...],
+            lower.astype(F32), -dt * rate,
             precision=lax.Precision.HIGHEST, preferred_element_type=F32,
         )
         cumul_t = cumul.T
@@ -85,7 +93,7 @@
                     weighting, drive16[:, h * size : (h + 1) * size], preferred_element_type=F32
                 )
             )
-        y_ref[b] = y + jnp.concatenate(parts, axis=1)
+        y_ref[b] = (y + jnp.concatenate(parts, axis=1)).astype(BF16)
         to_end = per_head(jnp.exp(last - cumul), heads, size)
         added = lax.dot_general(
             (to_end * drive).astype(BF16), bmat, (((0,), (0,)), ((), ())),
@@ -97,11 +105,15 @@
             held[b, at, :] = keep * held[b, at, :] + added[at, :]
         grow_ref[b] = jnp.exp(cumul + passed[b, 0:1, :])
         passed[b] = passed[b] + last
-    sec_ref[...] = held[...]
-    total_ref[...] = jnp.exp(passed[...])
-
-
-def scan_section(proj, before, taps, bias, rate, start, heads, inner, state):
+
+    @pl.when(i == pl.num_programs(0) - 1)
+    def _():
+        for b in range(batch):
+            high, low = high_low(jnp.exp(passed[b]))
+            sent_ref[b] = jnp.concatenate([held[b].astype(BF16), high, low], axis=0)
+
+
+def scan_section(proj, before, value_taps, bc_taps, bias, rate, cached, heads, inner, state):
     batch, length = proj.shape[:2]
     mix = inner + 2 * state
     step_at = mix // LANES
@@ -114,24 +126,23 @@
             rows(mix),
             rows(LANES, step_at),
             whole((batch, 16, mix)),
-            whole((CONV, mix)),
-            whole((1, LANES)),
-            whole((1, LANES)),
+            whole((CONV, inner)),
+            whole((CONV, 2 * state)),
+            pl.BlockSpec(memory_space=pltpu.SMEM),
+            pl.BlockSpec(memory_space=pltpu.SMEM),
             pl.BlockSpec(memory_space=pltpu.SMEM),
         ],
         out_specs=[
             rows(inner),
             rows(state),
             rows(LANES),
-            whole((batch, inner, state)),
-            whole((batch, 8, LANES)),
+            whole((batch, inner + 16, state)),
         ],
         out_shape=[
-            jax.ShapeDtypeStruct((batch, length, inner), F32),
+            jax.ShapeDtypeStruct((batch, length, inner), BF16),
             jax.ShapeDtypeStruct((batch, length, state), BF16),
             jax.ShapeDtypeStruct((batch, length, LANES), F32),
-            jax.ShapeDtypeStruct((batch, inner, state), F32),
-            jax.ShapeDtypeStruct((batch, 8, LANES), F32),
+            jax.ShapeDtypeStruct((batch, inner + 16, state), BF16),
         ],
         scratch_shapes=[
             pltpu.VMEM((batch, 8, mix), F32),
@@ -143,7 +154,7 @@
             transcendentals=batch * length * 2048,
         ),
         name="section_scan",
-    )(proj, proj, before, taps, bias, rate, start)
+    )(proj, proj, before, value_taps, bc_taps, bias, rate, cached)
 
 
 def remote(src, dst, send_sem, recv_sem, axis, index):
@@ -425,7 +436,7 @@
 
 def mix_kernel(
     pieces, heads, y_ref, c_ref, grow_ref, gate_ref, sent_ref, pool_ref, gain_ref, w_ref,
-    owner_ref, start_ref, out_ref, sums_ref,
+    owner_ref, cached_ref, out_ref, sums_ref,
     got, x, sq, states, incoming, left_sem, right_sem, side_sem, recv,
     sq_send, sq_recv, own_sem, st_send, st_recv,
 ):
@@ -472,9 +483,9 @@
             c_ref[at, :], incoming[b].astype(BF16), (((1,), (1,)), ((), ())),
             preferred_element_type=F32,
         )
-        y = y_ref[at, :] + per_head(grow_ref[at, :], heads, size) * carry
-        line = lax.broadcasted_iota(jnp.int32, (rows, inner), 0) + (j * rows - b * length)
-        y = jnp.where(line >= start_ref[b], y, 0.0)
+        y = y_ref[at, :].astype(F32) + per_head(grow_ref[at, :], heads, size) * carry
+        line = lax.broadcasted_iota(jnp.int32, (rows, inner), 0) + (sec * length + j * rows - b * length)
+        y = jnp.where(line >= cached_ref[b], y, 0.0)
         gated = y * silu(gate_ref[at, :].astype(F32))
         x[at, :] = (gated * gain_ref[...]).astype(BF16)
         sq[pl.ds(j, 1), :] = lax.dot_general(
@@ -608,30 +619,23 @@
     slots = kept_states.shape[0]
     n_seq = lax.axis_size("seq")
     n_head = lax.axis_size("head")
-    sec = lax.axis_index("seq")
-
     tokens_all = batch * sec_len
-    taps = jnp.concatenate([conv_value, conv_bc], axis=1)
-    bias = jnp.pad(step_bias, (0, LANES - heads))[None]
-    rates = jnp.pad(rate, (0, LANES - heads))[None]
     picked = jnp.stack(
         [lax.dynamic_index_in_dim(kept_states, kept_index[b] % slots, 0, False) for b in range(batch)]
     ).astype(BF16).reshape(batch, inner, state)
-    start = cached_len - sec * sec_len
     owner = (jnp.arange(n_seq)[:, None] == (kept_index // slots)[None, :]).astype(F32)
 
     mixin, gate, w_cols, before, pool = gather_project(
         tokens.reshape(tokens_all, d_part), w_value, w_bc,
         jnp.pad(w_step, ((0, 0), (0, LANES - heads))), w_gate, w_out, picked,
     )
-    y, cmat, grow, sec_state, total = scan_section(
-        mixin.reshape(batch, sec_len, -1), before, taps, bias, rates, start, heads, inner, state
+    y, cmat, grow, sent = scan_section(
+        mixin.reshape(batch, sec_len, -1), before, conv_value, conv_bc, step_bias, rate, cached_len,
+        heads, inner, state,
     )
-    high, low = high_low(total)
-    sent = jnp.concatenate([sec_state.astype(BF16), high, low], axis=1)
     mixed, sums = gather_mix(
         y.reshape(tokens_all, inner), cmat.reshape(tokens_all, state),
-        grow.reshape(tokens_all, LANES), gate, sent, pool, norm_gain[None], w_cols, owner, start,
+        grow.reshape(tokens_all, LANES), gate, sent, pool, norm_gain[None], w_cols, owner, cached_len,
         heads,
     )
     meansq = jnp.sum(sums, axis=0).reshape(-1) / (inner * n_head)

time: 292 us -> 287 us (0.983)
  other arithmetic: 9.39 us -> 5.2 us
where the time goes in v4:
time: 287 us
  Pallas kernels  269 us (94%)
  local copies, waits for them, and re-layouts  9.2 us (3%)
  other arithmetic  5.2 us (2%)
  between operations  4.01 us (1%)
    pallas_call x1, Pallas kernels, gather_project(): pl.pallas_call(functools.partial(project_kernel, pieces, batch, inner), i...  164 us
    pallas_call x1, Pallas kernels, gather_mix(): pl.pallas_call(functools.partial(mix_kernel, pieces, heads), in_specs=[VM...  89 us
    pallas_call x1, Pallas kernels, scan_section(): pl.pallas_call(functools.partial(scan_kernel, heads, inner, state), grid=...  15.7 us

profile of v4, /device:TPU:6, one launch (start us, length us, event | category | flops | bytes accessed | tf_op | source)
XLA Modules:
  0.0 286.9 jit_solution(9459367108994187209)
XLA Ops:
  0.0 0.7 and_select_fusion
  0.7 1.3 fusion.1
  5.9 1.0 dynamic-slice_convert_fusion.1
  6.9 0.7 pad_maximum_fusion.kept_ref
  7.6 1.3 copy.16
  8.8 1.2 pad.4.clone
  10.0 163.8 %gather_project.1 = (bf16[2048,640]{1,0:T(8,128)(2,1)}, bf16[2048,256]{1,0:T(8,128)(2,1)}, bf16[4,8,64,512]{3,2,1,0:T(8,128)(2,1)}, bf16[2,16,512]{2,1,0:T(8,128)(2,1)}, bf16[4,2,256,128]{3,2,1,0:T(8,128)(2,1)}) custom-call(bf16[2048,512]{1,0:T(8,128)(2,1)} %bitcast.23, bf16[8,512,256]{2,1,0:T(8,128)(2,1)} %bitcast.24, bf16[8,512,256]{2,1,0:T(8,128)(2,1)} %bitcast.25, ...), custom_call_target="tpu_custom_call" | custom-call | tf_op jit(solution)/shard_map/gather_project/pallas_call | solution.py:550
  173.8 0.0 copy-start
  173.8 0.0 copy-start.3
  173.8 0.0 copy-start.6
  173.8 0.0 copy-start.7
  173.9 15.7 %section_scan.1 = (bf16[2,1024,256]{2,1,0:T(8,128)(2,1)}, bf16[2,1024,128]{2,1,0:T(8,128)(2,1)}, f32[2,1024,128]{2,1,0:T(8,128)}, bf16[2,272,128]{2,1,0:T(8,128)(2,1)}) custom-call(bf16[2,1024,640]{2,1,0:T(8,128)(2,1)} %bitcast.30, bf16[2,1024,640]{2,1,0:T(8,128)(2,1)} %bitcast.31, bf16[2,16,512]{2,1,0:T(8,128)(2,1)} %get-tuple-element.17.before_ref, ...), custom_call_target="tpu_custom_call" | custom-call | flops 536870912 | bytes 8388608 | tf_op jit(solution)/shard_map/section_scan/pallas_call | solution.py:122
  189.6 0.0 copy-done
  189.6 0.0 copy-done.3
  189.6 0.0 copy-done.6
  189.6 0.0 copy-done.7
  189.6 0.0 copy-start.1
  189.6 1.2 copy-done.1
  190.8 0.0 copy-start.2
  190.8 1.2 copy-done.2
  192.1 1.0 copy-done.4
  193.1 0.9 copy-done.5
  194.0 89.0 %gather_mix.1 = (f32[2048,512]{1,0:T(8,128)}, f32[8,8,256]{2,1,0:T(8,128)S(1)}) custom-call(bf16[2048,256]{1,0:T(8,128)(2,1)S(1)} %bitcast.18, bf16[2048,128]{1,0:T(8,128)(2,1)S(1)} %bitcast.20, f32[2048,128]{1,0:T(8,128)S(1)} %bitcast.19, bf16[2048,256]{1,0:T(8,128)(2,1)S(1)} %copy-done, bf16[2,272,128]{2,1,0:T(8,128)(2,1)S(1)} %copy-done.5, ...), custom_call_target="tpu_custom_call" | custom-call | tf_op jit(solution)/shard_map/gather_mix/pallas_call | solution.py:580
  283.1 3.8 %multiply_convert_fusion = bf16[2048,512]{1,0:T(8,128)(2,1)} fusion(f32[2048,512]{1,0:T(8,128)} %get-tuple-element.25, f32[2048]{0:T(1024)S(1)} %bitcast.29), kind=kLoop, calls=%fused_computation | loop fusion | flops 2097152 | bytes 6299648 | tf_op jit(solution)/shard_map/convert_element_type | solution.py:642
  (6 shorter events, 0.0 us)
Async XLA Ops:
  173.8 15.8 %copy-start = (bf16[2048,256]{1,0:T(8,128)(2,1)S(1)}, bf16[2048,256]{1,0:T(8,128)(2,1)}, u32[]{:S(2)}) copy-start(bf16[2048,256]{1,0:T(8,128)(2,1)} %get-tuple-element.21.gate_ref) | copy-start | bytes 3145732
  173.8 15.8 %copy-start.3 = (bf16[4,2,256,128]{3,2,1,0:T(8,128)(2,1)S(1)}, bf16[4,2,256,128]{3,2,1,0:T(8,128)(2,1)}, u32[]{:S(2)}) copy-start(bf16[4,2,256,128]{3,2,1,0:T(8,128)(2,1)} %get-tuple-element.23.pool_ref) | copy-start | bytes 1572868
  173.8 15.8 %copy-start.6 = (f32[256]{0:T(256)S(1)}, f32[256]{0:T(256)}, u32[]{:S(2)}) copy-start(f32[256]{0:T(256)} %param.23) | copy-start | bytes 3076
  173.8 15.8 %copy-start.7 = (s32[2]{0:T(128)S(1)}, s32[2]{0:T(128)}, u32[]{:S(2)}) copy-start(s32[2]{0:T(128)} %cached_ref.3) | copy-start | bytes 28
  189.6 1.2 copy-start.1
  190.8 1.2 copy-start.2
  192.1 1.0 copy-start.4
  193.1 0.9 copy-start.5
